TPU v7x, 256 devices: a whole 4x4x8 slice. The times are simulated.
256 devices in a mesh: zone: 8 (over x, core), sub: 8 (over z), row: 4 (over y).
Axes of the slice: x: 4, y: 4, z: 8, core: 2. Of those that a mesh axis runs over, the one named last changes fastest.
Arguments:
- z_inverse: bfloat16 [64, 2048, 2048], P(('zone', 'sub'), 'row'), may hold values from -2 to 2
- sources: bfloat16 [4, 64, 2048, 512], P(None, ('zone', 'sub'), 'row'), may hold values from -6 to 6
- v_start: float32 [64, 2048, 512], P(('zone', 'sub'), 'row'), may hold values from -6 to 6
- hist_near: float32 [2, 64, 256, 512], P(None, ('zone', 'sub'), 'row'), may hold values from -6 to 6
- hist_far: float32 [2, 64, 256, 512], P(None, ('zone', 'sub'), 'row'), may hold values from -6 to 6
- switch_on: int32 [4, 64, 2048], P(None, ('zone', 'sub'), 'row'), may hold values 0 or 1
- switch_cond: float32 [64, 2048], P(('zone', 'sub'), 'row'), may hold values from 0.1 to 1
- fault_node: int32 [512], replicated, may hold values from 0 to 2047
- fault_cond: float32 [512], replicated, may hold values from 0.2 to 1.5
- remote_sub: int32 [64, 256, 1], P(('zone', 'sub'), 'row'), may hold values from 0 to 63; in each aligned block of 64 rows (0 to 63, 64 to 127, ..., all dimensions but the last counted through in order) at most 2 rows name the same one
- near_node: int32 [64, 256], P(('zone', 'sub'), 'row'), may hold values from 0 to 511
- far_node: int32 [64, 256], P(('zone', 'sub'), 'row'), may hold values from 0 to 511
- line_gain: float32 [64, 256], P(('zone', 'sub'), 'row'), may hold values from 0.3 to 1.5
Outputs:
- v_last: float32 [64, 2048, 512], P(('zone', 'sub'), 'row')
All inputs are finite; a program needn't handle non-finite values. No bound on the sum of `switch_on` on one device may be relied on, other than what follows from the above.
Results may differ from a plain program's by a relative error of at most 0.0034.
Values may be sent and summed in bfloat16 or wider, within the bound.
A program may use at most 64 MiB of HBM per device.

v0:
```python
import jax
import jax.numpy as jnp
from jax import lax
from jax.sharding import PartitionSpec as P


def send_nodes(buffer):
    return lax.all_to_all(buffer, ("zone", "sub"), split_axis=0, concat_axis=0, tiled=True)


def send_lines(buffer):
    return lax.all_to_all(buffer, ("zone", "sub"), split_axis=0, concat_axis=0, tiled=True)


def local(
    z_inverse,
    sources,
    v_start,
    hist_near,
    hist_far,
    switch_on,
    switch_cond,
    fault_node,
    fault_cond,
    remote_sub,
    near_node,
    far_node,
    line_gain,
):
    inverse_rows = z_inverse[0]
    rows = inverse_rows.shape[0]
    cases = sources.shape[3]
    steps = sources.shape[0]
    zones = lax.axis_size("zone")
    subs = lax.axis_size("sub")
    owners = zones * subs
    lines = near_node.shape[1]
    capacity = max(2, 2 * lines // owners)
    row_start = lax.axis_index("row") * rows
    target = remote_sub[0, :, 0]
    order = jnp.arange(lines, dtype=jnp.int32)
    before = (target[None, :] == target[:, None]) & (order[None, :] < order[:, None])
    rank = jnp.sum(before.astype(jnp.int32), axis=1)
    slot = target * capacity + rank
    node_a = near_node[0]
    outgoing_nodes = jnp.full((owners * capacity,), -1, jnp.int32).at[slot].set(far_node[0])
    incoming_nodes = send_nodes(outgoing_nodes)
    valid = incoming_nodes >= 0
    drop_index = jnp.where(valid, incoming_nodes, rows)
    read_index = jnp.clip(incoming_nodes, 0, rows - 1)
    all_index = jnp.concatenate([node_a, drop_index])
    gain = line_gain[0][:, None]
    global_rows = row_start + jnp.arange(rows, dtype=jnp.int32)
    fault_mask = (global_rows[:, None] == fault_node[None, :]).astype(jnp.float32)
    fault_term = fault_mask * fault_cond[None, :]
    conduct = switch_cond[0][:, None]
    v_prev = v_start[0]
    near_list, far_list, vn_list, vf_list = ([], [], [], [])
    for step in range(steps):
        if step < 2:
            near_h = hist_near[step, 0]
            far_h = hist_far[step, 0]
        else:
            far_h = gain * vn_list[step - 2] - near_list[step - 2]
            near_h = gain * vf_list[step - 2] - far_list[step - 2]
        near_list.append(near_h)
        far_list.append(far_h)
        arrived = send_lines(jnp.zeros((owners * capacity, cases), jnp.float32).at[slot].set(far_h))
        values = jnp.concatenate([near_h, arrived], axis=0)
        lines_in = jnp.zeros((rows, cases), jnp.float32).at[all_index].add(values, mode="drop")
        switched = switch_on[step, 0][:, None].astype(jnp.float32) * conduct
        inj = (
            sources[step, 0].astype(jnp.float32)
            + lines_in
            - switched * v_prev
            - fault_term * v_prev
        )
        injb = inj.astype(jnp.bfloat16)
        volts = jnp.dot(
            inverse_rows,
            lax.all_gather(injb, "row", axis=0, tiled=True),
            preferred_element_type=jnp.float32,
        )
        if step < steps - 2:
            near_volts = volts[node_a]
            vn_list.append(near_volts)
            reply = jnp.where(valid[:, None], volts[read_index], 0.0)
            returned = send_lines(reply)
            vf_list.append(returned[slot])
        v_prev = volts
    return v_prev[None]


def solution(mesh):
    placed = (
        P(("zone", "sub"), "row", None),
        P(None, ("zone", "sub"), "row", None),
        P(("zone", "sub"), "row", None),
        P(None, ("zone", "sub"), "row", None),
        P(None, ("zone", "sub"), "row", None),
        P(None, ("zone", "sub"), "row"),
        P(("zone", "sub"), "row"),
        P(),
        P(),
        P(("zone", "sub"), "row", None),
        P(("zone", "sub"), "row"),
        P(("zone", "sub"), "row"),
        P(("zone", "sub"), "row"),
    )
    return jax.shard_map(
        local,
        mesh=mesh,
        in_specs=placed,
        out_specs=P(("zone", "sub"), "row", None),
        check_vma=False,
    )
```

profile of v0, /device:TPU:8, one launch (start us, length us, event | category | flops | bytes accessed | tf_op | source)
XLA Modules:
  0.0 272.6 jit_solution(11945253763654875632)
XLA Ops:
  9.9 12.2 %all-to-all-start = ((s32[64,2,1]{1,2,0:T(1,128)}), s32[64,2,1]{1,2,0:T(1,128)}, u32[]{:S(2)}, u32[]{:S(2)}) async-start(s32[64,2,1]{1,2,0:T(1,128)} %bitcast.7), calls=%async_computation | async-start | bytes 65536 | tf_op jit(solution)/shard_map/all_to_all | solution.py:8
  22.1 3.8 %bitcast_convert_fusion = (f32[512,512]{1,0:T(8,128)}, f32[512,512]{1,0:T(8,128)}, f32[512,512]{1,0:T(8,128)}, f32[512,512]{1,0:T(8,128)}) fusion(bf16[4,1,512,512]{3,2,1,0:T(8,128)(2,1)} %param.14), kind=kLoop, calls=%fused_computation.41 | loop fusion | flops 1048576 | bytes 6291456 | tf_op jit(solution)/shard_map/convert_element_type | solution.py:73
  29.0 1.6 copy.62
  31.5 9.5 %all-to-all-start.2 = ((f32[64,2,512]{2,1,0:T(2,128)}), f32[64,2,512]{2,1,0:T(2,128)}, u32[]{:S(2)}, u32[]{:S(2)}) async-start(f32[64,2,512]{2,1,0:T(2,128)} %all_to_all.58), calls=%async_computation.2 | async-start | bytes 524288 | tf_op jit(solution)/shard_map/all_to_all | solution.py:12
  41.7 2.2 clamp_reduce_fusion
  43.9 1.5 all_to_all.54
  46.0 1.3 compare_select_fusion
  47.3 6.8 %all-to-all-done.2 = f32[64,2,512]{2,1,0:T(2,128)} async-done(((f32[64,2,512]{2,1,0:T(2,128)}), f32[64,2,512]{2,1,0:T(2,128)}, u32[]{:S(2)}, u32[]{:S(2)}) %all-to-all-start.2) | async-done | bytes 262176 | tf_op jit(solution)/shard_map/all_to_all | solution.py:12
  54.1 1.8 all_to_all.60
  55.9 4.3 %scatter_custom_fusion.4 = f32[512,512]{1,0:T(8,128)} fusion(f32[512,512]{1,0:T(8,128)} %get-tuple-element.10, s32[192]{0:T(256)} %bitcast.111, f32[128,512]{1,0:T(8,128)} %all_to_all.60, f32[]{:T(128)} %constant.42, f32[64,512]{1,0:T(8,128)} %get-tuple-element.14), kind=kCustom, calls=%fused_computation.49 | custom fusion | flops 196608 | bytes 1442304 | tf_op jit(solution)/shard_map/scatter-add | solution.py:70
  60.3 2.6 copy.63
  62.8 2.3 fusion.21
  65.2 1.9 scatter_custom_fusion.1
  67.1 1.8 all_to_all.55
  69.0 18.6 %all_to_all.78 = f32[64,2,512]{2,1,0:T(2,128)} all-to-all(f32[64,2,512]{2,1,0:T(2,128)} %all_to_all.55), channel_id=1, replica_groups=mesh['zone'=8,'sub'=8,'row'=4] {'zone','sub'}, dimensions={0} | all-to-all | bytes 524288 | tf_op jit(solution)/shard_map/all_to_all | solution.py:12
  87.5 1.9 all_to_all.57
  89.4 2.6 scatter_custom_fusion.2
  92.0 1.3 copy.64
  93.6 4.3 %fusion.23 = (bf16[512,512]{0,1:T(8,128)(2,1)}, f32[512,512]{0,1:T(8,128)}) fusion(f32[512,512]{0,1:T(8,128)} %copy.64, f32[512]{0:T(512)S(1)} %copy-done.7, s32[512]{0:T(512)S(1)} %iota_add_fusion, f32[512]{0:T(512)S(1)} %copy-done.14, s32[512]{0:T(512)S(1)} %copy-done.8, bf16[2048,512]{0,1:T(8,128)(2,1)} %all-gather.5.cloned.1.call-done, ...), kind=kOutput, calls=%fused_computation.34 | convolution fusion | flops 1075576832 | bytes 6823936 | tf_op jit(solution)/shard_map/dot_general | solution.py:79
  99.2 1.6 copy.67
  100.7 1.5 gather_fusion.2
  102.2 1.8 gather.27
  104.0 1.7 scatter_custom_fusion.7
  105.7 1.8 all_to_all.68
  107.5 10.9 %all-to-all-start.6 = ((f32[64,2,512]{2,1,0:T(2,128)}), f32[64,2,512]{2,1,0:T(2,128)}, u32[]{:S(2)}, u32[]{:S(2)}) async-start(f32[64,2,512]{2,1,0:T(2,128)} %all_to_all.68), calls=%async_computation.6 | async-start | bytes 524288 | tf_op jit(solution)/shard_map/all_to_all | solution.py:12
  118.4 13.1 %all-gather.7.cloned.1.call-done = bf16[2048,512]{0,1:T(8,128)(2,1)} async-done(((bf16[512,512]{0,1:T(8,128)(2,1)}), bf16[2048,512]{0,1:T(8,128)(2,1)}) %all-gather.7.cloned.1.call-update) | async-done | bytes 2097168 | tf_op jit(solution)/shard_map/all_gather | solution.py:81
  131.5 3.9 %fusion.11 = f32[512,512]{0,1:T(8,128)} fusion(bf16[2048,512]{0,1:T(8,128)(2,1)} %all-gather.7.cloned.1.call-done, bf16[1,512,2048]{2,1,0:T(8,128)(2,1)S(1)} %copy-done), kind=kOutput, calls=%fused_computation.28 | convolution fusion | flops 1073741824 | bytes 5242880 | tf_op jit(solution)/shard_map/dot_general | solution.py:79
  135.4 1.6 copy.65
  138.5 2.0 broadcast_select_fusion
  140.6 23.6 %all_to_all.79 = f32[64,2,512]{2,1,0:T(2,128)} all-to-all(f32[64,2,512]{2,1,0:T(2,128)S(1)} %get-tuple-element.20), channel_id=1, replica_groups=mesh['zone'=8,'sub'=8,'row'=4] {'zone','sub'}, dimensions={0} | all-to-all | bytes 524288 | tf_op jit(solution)/shard_map/all_to_all | solution.py:12
  164.1 5.5 %all-to-all-start.5 = ((f32[64,2,512]{2,1,0:T(2,128)}), f32[64,2,512]{2,1,0:T(2,128)}, u32[]{:S(2)}, u32[]{:S(2)}) async-start(f32[64,2,512]{2,1,0:T(2,128)} %get-tuple-element.19), calls=%async_computation.5 | async-start | bytes 524288 | tf_op jit(solution)/shard_map/all_to_all | solution.py:12
  170.2 1.8 all_to_all.70
  174.0 8.7 %all-to-all-done.5 = f32[64,2,512]{2,1,0:T(2,128)} async-done(((f32[64,2,512]{2,1,0:T(2,128)}), f32[64,2,512]{2,1,0:T(2,128)}, u32[]{:S(2)}, u32[]{:S(2)}) %all-to-all-start.5) | async-done | bytes 262176 | tf_op jit(solution)/shard_map/all_to_all | solution.py:12
  182.7 1.1 all_to_all.67
  183.8 1.4 gather_fusion.3
  185.2 1.8 bitcast_subtract_fusion
  187.0 4.3 %scatter_custom_fusion.8 = f32[512,512]{1,0:T(8,128)} fusion(f32[512,512]{1,0:T(8,128)} %get-tuple-element.7, s32[192]{0:T(256)} %bitcast.113, f32[128,512]{1,0:T(8,128)} %all_to_all.70, f32[]{:T(128)} %constant.42, f32[64,512]{1,0:T(8,128)S(1)} %get-tuple-element.11), kind=kCustom, calls=%fused_computation.57 | custom fusion | flops 196608 | bytes 1442304 | tf_op jit(solution)/shard_map/scatter-add | solution.py:70
  191.3 2.5 copy.69
  193.8 2.7 fusion.25
  196.6 1.8 scatter_custom_fusion.5
  199.5 17.9 %all_to_all.80 = f32[64,2,512]{2,1,0:T(2,128)S(1)} all-to-all(f32[64,2,512]{2,1,0:T(2,128)S(1)} %all_to_all.63), channel_id=1, replica_groups=mesh['zone'=8,'sub'=8,'row'=4] {'zone','sub'}, dimensions={0} | all-to-all | bytes 524288 | tf_op jit(solution)/shard_map/all_to_all | solution.py:12
  217.6 4.0 %scatter_custom_fusion.6 = f32[512,512]{1,0:T(8,128)} fusion(f32[512,512]{1,0:T(8,128)} %get-tuple-element.9, s32[192]{0:T(256)} %bitcast.114, f32[128,512]{1,0:T(8,128)S(1)} %all_to_all.65, f32[]{:T(128)} %constant.42, f32[64,512]{1,0:T(8,128)S(1)} %copy-done.5), kind=kCustom, calls=%fused_computation.53 | custom fusion | flops 196608 | bytes 1442304 | tf_op jit(solution)/shard_map/scatter-add | solution.py:70
  221.6 1.6 copy.70
  223.2 1.3 all-gather.9.cloned.1.call-done
  224.5 3.7 %fusion.27 = bf16[512,512]{0,1:T(8,128)(2,1)} fusion(f32[512,512]{0,1:T(8,128)S(1)} %copy.70, bf16[2048,512]{0,1:T(8,128)(2,1)} %all-gather.9.cloned.1.call-done, bf16[1,512,2048]{2,1,0:T(8,128)(2,1)S(1)} %copy-done, f32[512]{0:T(512)S(1)} %copy-done.13, f32[512]{0:T(512)S(1)} %copy-done.7, s32[512]{0:T(512)S(1)} %iota_add_fusion, s32[512]{0:T(512)S(1)} %copy-done.8), kind=kOutput, calls=%fused_computation.38 | convolution fusion | flops 1075576832 | bytes 5775360 | tf_op jit(solution)/shard_map/dot_general | solution.py:79
  228.3 33.6 %all-gather.11.cloned.1.call-done = bf16[2048,512]{0,1:T(8,128)(2,1)} async-done(((bf16[512,512]{0,1:T(8,128)(2,1)}), bf16[2048,512]{0,1:T(8,128)(2,1)}) %all-gather.11.cloned.1.call-update) | async-done | bytes 2097168 | tf_op jit(solution)/shard_map/all_gather | solution.py:81
  261.9 2.9 %fusion.17 = f32[1,512,512]{1,2,0:T(8,128)S(1)} fusion(bf16[2048,512]{0,1:T(8,128)(2,1)} %all-gather.11.cloned.1.call-done, bf16[1,512,2048]{2,1,0:T(8,128)(2,1)S(1)} %copy-done), kind=kOutput, calls=%fused_computation.30 | convolution fusion | flops 1073741824 | bytes 5242880 | tf_op jit(solution)/shard_map/dot_general | solution.py:79
  264.7 1.3 copy.71
  (74 shorter events, 15.7 us)
Async XLA Ops:
  6.5 87.0 %copy-start = (bf16[1,512,2048]{2,1,0:T(8,128)(2,1)S(1)}, bf16[1,512,2048]{2,1,0:T(8,128)(2,1)}, u32[]{:S(2)}) copy-start(bf16[1,512,2048]{2,1,0:T(8,128)(2,1)} %param.13) | copy-start | bytes 6291460
  8.2 19.0 %copy-start.15 = (s32[64]{0:T(128)}, s32[64]{0:T(128)S(1)}, u32[]{:S(2)}) copy-start(s32[64]{0:T(128)S(1)} %fusion.66) | copy-start | bytes 772
  9.9 21.7 %all-to-all-start = ((s32[64,2,1]{1,2,0:T(1,128)}), s32[64,2,1]{1,2,0:T(1,128)}, u32[]{:S(2)}, u32[]{:S(2)}) async-start(s32[64,2,1]{1,2,0:T(1,128)} %bitcast.7), calls=%async_computation | async-start | bytes 65536 | tf_op jit(solution)/shard_map/all_to_all | solution.py:8
  22.1 3.9 %copy-start.2 = (f32[2,1,64,512]{3,2,1,0:T(8,128)S(1)}, f32[2,1,64,512]{3,2,1,0:T(8,128)}, u32[]{:S(2)}) copy-start(f32[2,1,64,512]{3,2,1,0:T(8,128)} %param.16) | copy-start | bytes 786436
  22.1 4.5 %copy-start.10 = (s32[4,1,512]{2,1,0:T(1,128)S(1)}, s32[4,1,512]{2,1,0:T(1,128)}, u32[]{:S(2)}) copy-start(s32[4,1,512]{2,1,0:T(1,128)} %param.18) | copy-start | bytes 24580
  22.1 4.5 %copy-start.12 = (f32[1,512]{1,0:T(1,128)S(1)}, f32[1,512]{1,0:T(1,128)}, u32[]{:S(2)}) copy-start(f32[1,512]{1,0:T(1,128)} %param.19) | copy-start | bytes 6148
  22.1 5.1 %copy-start.4 = (f32[2,1,64,512]{3,2,1,0:T(8,128)S(1)}, f32[2,1,64,512]{3,2,1,0:T(8,128)}, u32[]{:S(2)}) copy-start(f32[2,1,64,512]{3,2,1,0:T(8,128)} %param.17) | copy-start | bytes 786436
  31.5 22.6 %all-to-all-start.2 = ((f32[64,2,512]{2,1,0:T(2,128)}), f32[64,2,512]{2,1,0:T(2,128)}, u32[]{:S(2)}, u32[]{:S(2)}) async-start(f32[64,2,512]{2,1,0:T(2,128)} %all_to_all.58), calls=%async_computation.2 | async-start | bytes 524288 | tf_op jit(solution)/shard_map/all_to_all | solution.py:12
  41.0 52.5 %all-gather.5.cloned.1.call-start = ((), (), s32[]{:S(2)}) async-start(), calls=%async_computation.7 | async-start | bytes 2621440 | tf_op jit(solution)/shard_map/all_gather | solution.py:81
  41.7 21.2 %copy-start.7 = (f32[512]{0:T(512)S(1)}, f32[512]{0:T(512)}, u32[]{:S(2)}) copy-start(f32[512]{0:T(512)} %param.21) | copy-start | bytes 6148
  41.7 21.2 %copy-start.8 = (s32[512]{0:T(512)S(1)}, s32[512]{0:T(512)}, u32[]{:S(2)}) copy-start(s32[512]{0:T(512)} %param.20) | copy-start | bytes 6148
  65.1 24.3 %copy-start.1 = (f32[512,512]{1,0:T(8,128)S(1)}, f32[512,512]{1,0:T(8,128)}, u32[]{:S(2)}) copy-start(f32[512,512]{1,0:T(8,128)} %get-tuple-element.8) | copy-start | bytes 3145732
  65.2 66.3 %all-gather.7.cloned.1.call-start = ((), (), s32[]{:S(2)}) async-start(), calls=%async_computation.8 | async-start | bytes 2621440 | tf_op jit(solution)/shard_map/all_gather | solution.py:81
  87.5 6.0 %copy-start.14 = (f32[512]{0:T(512)S(1)}, f32[512]{0:T(512)}, u32[]{:S(2)}) copy-start(f32[512]{0:T(512)} %get-tuple-element.24) | copy-start | bytes 6148
  93.5 4.4 %copy-start.17 = (s32[1,64]{1,0:T(1,128)S(1)}, s32[1,64]{1,0:T(1,128)}, u32[]{:S(2)}) copy-start(s32[1,64]{1,0:T(1,128)} %param.23) | copy-start | bytes 772
  93.5 4.4 %copy-start.6 = (s32[64,2]{1,0:T(8,128)S(1)}, s32[64,2]{1,0:T(8,128)}, u32[]{:S(2)}) copy-start(s32[64,2]{1,0:T(8,128)} %get-tuple-element.5) | copy-start | bytes 1540
  99.1 4.9 %copy-start.11 = (f32[1,64]{1,0:T(1,128)S(1)}, f32[1,64]{1,0:T(1,128)}, u32[]{:S(2)}) copy-start(f32[1,64]{1,0:T(1,128)} %param.25) | copy-start | bytes 772
  99.1 4.9 %copy-start.16 = (s32[64]{0:T(128)S(1)}, s32[64]{0:T(128)}, u32[]{:S(2)}) copy-start(s32[64]{0:T(128)} %copy-done.15) | copy-start | bytes 772
  107.5 33.0 %all-to-all-start.6 = ((f32[64,2,512]{2,1,0:T(2,128)}), f32[64,2,512]{2,1,0:T(2,128)}, u32[]{:S(2)}, u32[]{:S(2)}) async-start(f32[64,2,512]{2,1,0:T(2,128)} %all_to_all.68), calls=%async_computation.6 | async-start | bytes 524288 | tf_op jit(solution)/shard_map/all_to_all | solution.py:12
  164.1 18.5 %all-to-all-start.5 = ((f32[64,2,512]{2,1,0:T(2,128)}), f32[64,2,512]{2,1,0:T(2,128)}, u32[]{:S(2)}, u32[]{:S(2)}) async-start(f32[64,2,512]{2,1,0:T(2,128)} %get-tuple-element.19), calls=%async_computation.5 | async-start | bytes 524288 | tf_op jit(solution)/shard_map/all_to_all | solution.py:12
  169.6 54.9 %all-gather.9.cloned.1.call-start = ((), (), s32[]{:S(2)}) async-start(), calls=%async_computation.9 | async-start | bytes 2621440 | tf_op jit(solution)/shard_map/all_gather | solution.py:81
  187.0 6.8 %copy-start.9 = (f32[512]{0:T(512)S(1)}, f32[512]{0:T(512)}, u32[]{:S(2)}) copy-start(f32[512]{0:T(512)} %get-tuple-element.22) | copy-start | bytes 6148
  193.8 2.7 %copy-start.3 = (f32[2,1,64,512]{3,2,1,0:T(8,128)S(1)}, f32[2,1,64,512]{3,2,1,0:T(8,128)}, u32[]{:S(2)}) copy-start(f32[2,1,64,512]{3,2,1,0:T(8,128)} %param.16) | copy-start | bytes 786436
  196.5 21.1 %copy-start.5 = (f32[64,512]{1,0:T(8,128)S(1)}, f32[64,512]{1,0:T(8,128)}, u32[]{:S(2)}) copy-start(f32[64,512]{1,0:T(8,128)} %get-tuple-element.12) | copy-start | bytes 393220
  196.5 65.3 %all-gather.11.cloned.1.call-start = ((), (), s32[]{:S(2)}) async-start(), calls=%async_computation.10 | async-start | bytes 2621440 | tf_op jit(solution)/shard_map/all_gather | solution.py:81
  217.4 7.1 %copy-start.13 = (f32[512]{0:T(512)S(1)}, f32[512]{0:T(512)}, u32[]{:S(2)}) copy-start(f32[512]{0:T(512)} %get-tuple-element.21) | copy-start | bytes 6148
Sparse Core Ops, SparseCore 0:
  65.3 28.2 all-gather.4
  98.0 33.4 all-gather.6
  196.6 27.8 all-gather.8
  228.4 33.4 all-gather.10
where the time goes:
time: 276 us; the launch traced here: 273 us
  waiting for transfers between devices  64.8 us (23%)
  blocking collectives  60 us (22%)
  local copies, waits for them, and re-layouts  42.1 us (15%)
  other arithmetic  39.2 us (14%)
  starting transfers between devices  38.2 us (14%)
  matrix products  14.8 us (5%)
  between operations  13.4 us (5%)
    all_to_all x3, blocking collectives, send_lines(): lax.all_to_all(buffer, ('zone', 'sub'), split_axis=0, concat_axis=0, tile...  60 us
    all_gather x4, waiting for transfers between devices, local(): lax.all_gather(injb, 'row', axis=0, tiled=True)  48.2 us
    all_to_all x3, starting transfers between devices, send_lines(): lax.all_to_all(buffer, ('zone', 'sub'), split_axis=0, concat_axis=0, tile...  25.8 us
    all_to_all x3, waiting for transfers between devices, send_lines(): lax.all_to_all(buffer, ('zone', 'sub'), split_axis=0, concat_axis=0, tile...  15.5 us
    scatter-add x4, other arithmetic, local(): jnp.zeros((rows, cases), jnp.float32).at[all_index].add(values, mode='drop')  15.2 us
    dot_general x4, matrix products, local(): jnp.dot(inverse_rows, lax.all_gather(injb, 'row', axis=0, tiled=True), pr...  14.8 us
    all_to_all x10, local copies, waits for them, and re-layouts, send_lines(): lax.all_to_all(buffer, ('zone', 'sub'), split_axis=0, concat_axis=0, tile...  13.5 us
    all_to_all x1, starting transfers between devices, send_nodes(): lax.all_to_all(buffer, ('zone', 'sub'), split_axis=0, concat_axis=0, tile...  12.2 us
  transfers between devices with their start and end apart: 8, of which 7 were waited for; matrix products, arithmetic and copies ran while one was open for 16% of the time, Pallas kernels for 0%

commit v1 on v0

v1 whole, which is shorter than its diff:
```python
import functools

import jax
import jax.numpy as jnp
from jax import lax
from jax.experimental import pallas as pl
from jax.experimental.pallas import tpu as pltpu
from jax.sharding import PartitionSpec as P

MESH = pl.DeviceIdType.MESH
F32 = jnp.float32
BF16 = jnp.bfloat16
GROUPS = 4
AHEAD = 1


def dot(a, b):
    return jnp.dot(a, b, preferred_element_type=F32)


def iota(shape, dim):
    return lax.broadcasted_iota(jnp.int32, shape, dim)


def one_hot(mask):
    return jnp.where(mask, 1.0, 0.0).astype(BF16)


def to_column(row, size):
    eye = iota((size, size), 0) == iota((size, size), 1)
    return jnp.sum(jnp.where(eye, row, 0.0), axis=1, keepdims=True)


def to_row(column, size):
    eye = iota((size, size), 0) == iota((size, size), 1)
    return jnp.sum(jnp.where(eye, column, 0.0), axis=0, keepdims=True)


def kernel(
    zones,
    subs,
    z_hbm,
    src_hbm,
    vs_hbm,
    near_hbm,
    far_hbm,
    switch_on,
    switch_cond,
    fault_node,
    fault_cond,
    remote_sub,
    near_node,
    far_node,
    line_gain,
    out_hbm,
    zr,
    x,
    v,
    src,
    hist_near,
    hist_far,
    switched,
    scatter,
    gather,
    slots_out,
    slots_back,
    swap,
    gain,
    rhs,
    oa0,
    ra0,
    ob0,
    rb0,
    oa1,
    ra1,
    ob1,
    rb1,
    oa2,
    ra2,
    ob2,
    rb2,
    oa,
    ra,
    ob,
    rb,
    load_sem,
    send_sem,
    left_sem,
    right_sem,
    far_sem,
    ex_send,
    ex_recv,
    out_sem,
):
    rows, nodes = z_hbm.shape
    steps, _, cases = src_hbm.shape
    lines = near_node.shape[1]
    slots = 2 * zones * subs
    block_a, block_b = 2 * zones, 2 * subs
    width = cases // GROUPS
    half = 2 * width
    items = steps * GROUPS
    my_zone, my_sub, me = (lax.axis_index(name) for name in ("zone", "sub", "row"))
    right, left, across = lax.rem(me + 1, 4), lax.rem(me + 3, 4), lax.rem(me + 2, 4)

    loads = [pltpu.make_async_copy(far_hbm, hist_far, load_sem.at[0])]
    loads.append(pltpu.make_async_copy(near_hbm, hist_near, load_sem.at[1]))
    loads.append(pltpu.make_async_copy(src_hbm, src, load_sem.at[2]))
    for g in range(GROUPS):
        loads.append(
            pltpu.make_async_copy(vs_hbm.at[:, pl.ds(g * width, width)], v.at[g], load_sem.at[3 + g])
        )
    for place, origin in enumerate((me, left, right, across)):
        columns = pl.ds(pl.multiple_of(origin * rows, rows), rows)
        loads.append(
            pltpu.make_async_copy(
                z_hbm.at[:, columns], zr.at[:, pl.ds(place * rows, rows)], load_sem.at[3 + GROUPS + place]
            )
        )
    for load in loads:
        load.start()

    barrier = pltpu.get_barrier_semaphore()
    for neighbour in (left, right):
        pl.semaphore_signal(barrier, inc=1, device_id={"row": neighbour}, device_id_type=MESH)
    for d in range(1, subs):
        pl.semaphore_signal(barrier, inc=1, device_id={"sub": lax.rem(my_sub + d, subs)}, device_id_type=MESH)
    for d in range(1, zones):
        pl.semaphore_signal(barrier, inc=1, device_id={"zone": lax.rem(my_zone + d, zones)}, device_id_type=MESH)

    target = remote_sub[...].astype(F32)
    target_col = to_column(target, lines)
    same = target_col == target
    first, second = iota((lines, lines), 0), iota((lines, lines), 1)
    rank = jnp.sum(jnp.where(same & (first < second), 1.0, 0.0), axis=0, keepdims=True)
    rank_col = jnp.sum(jnp.where(same & (second < first), 1.0, 0.0), axis=1, keepdims=True)
    target_int = remote_sub[...]
    zone_of = target_int // subs
    sub_of = target_int - zone_of * subs
    slot_a = sub_of * block_a + zone_of * 2 + rank.astype(jnp.int32)
    slot_b = (target_col * 2.0 + rank_col).astype(jnp.int32)
    slots_out[...] = one_hot(iota((slots, lines), 0) == slot_a)
    slots_back[...] = one_hot(iota((lines, slots), 1) == slot_b)
    k = iota((slots, slots), 0)
    z_of, rest = k // (2 * subs), k - (k // (2 * subs)) * (2 * subs)
    swap[...] = one_hot(iota((slots, slots), 1) == (rest // 2) * block_a + z_of * 2 + (rest - (rest // 2) * 2))
    far_col = (to_column(far_node[...].astype(F32), lines) + 1.0).astype(jnp.int32)
    high = far_col // 16
    numbers = jnp.where(iota((lines, 128), 1) < 64, high, far_col - high * 16).astype(F32).astype(BF16)
    numbers_out = dot(slots_out[...], numbers).astype(BF16)

    def send_subs(out, got, which):
        got[pl.ds(my_sub, 1)] = out[pl.ds(my_sub, 1)]

        def one(d, carry):
            partner = lax.rem(my_sub + d, subs)
            pltpu.make_async_remote_copy(
                src_ref=out.at[partner],
                dst_ref=got.at[my_sub],
                send_sem=ex_send.at[which, 0],
                recv_sem=ex_recv.at[which, 0],
                device_id={"sub": partner},
                device_id_type=MESH,
            ).start()
            return carry

        lax.fori_loop(1, subs, one, 0)

    def send_zones(out, got, which):
        got[pl.ds(my_zone, 1)] = out[pl.ds(my_zone, 1)]

        def one(d, carry):
            partner = lax.rem(my_zone + d, zones)
            pltpu.make_async_remote_copy(
                src_ref=out.at[partner],
                dst_ref=got.at[my_zone],
                send_sem=ex_send.at[which, 1],
                recv_sem=ex_recv.at[which, 1],
                device_id={"zone": partner},
                device_id_type=MESH,
            ).start()
            return carry

        lax.fori_loop(1, zones, one, 0)

    def all_of(buffer, which, phase, axis, size):
        part = buffer.at[pl.ds(0, size - 1)]
        return pltpu.make_async_remote_copy(
            src_ref=part,
            dst_ref=part,
            send_sem=ex_send.at[which, phase],
            recv_sem=ex_recv.at[which, phase],
            device_id={axis: 0},
            device_id_type=MESH,
        )

    def wait_subs(buffer, which):
        all_of(buffer, which, 0, "sub", subs).wait_recv()

    def wait_zones(buffer, which):
        all_of(buffer, which, 1, "zone", zones).wait_recv()

    def turn(got):
        values = got.reshape(slots, got.shape[-1])
        return dot(swap[...], values).astype(BF16).reshape(zones, block_b, got.shape[-1])

    loads[0].wait()
    spread = slots_out[...]
    for step in range(2):
        values = dot(spread, hist_far[step].astype(BF16)).astype(BF16)
        if step == 0:
            oa0[:, :, :half] = values[:, :half].reshape(subs, block_a, half)
            oa0[:, :, half:] = numbers_out.reshape(subs, block_a, 128)
            oa1[...] = values[:, half:].reshape(subs, block_a, half)
        else:
            oa2[...] = values.reshape(subs, block_a, cases)
        if step == 0:
            pl.semaphore_wait(barrier, 2 + subs - 1 + zones - 1)
            send_subs(oa0, ra0, 0)
            send_subs(oa1, ra1, 1)
        else:
            send_subs(oa2, ra2, 2)

    near_row = near_node[...]
    near_col = to_column(near_row.astype(F32), lines).astype(jnp.int32)
    near_matrix = one_hot(iota((rows, lines), 0) == near_row)
    scatter[:, :lines] = near_matrix
    scatter[:, lines : 2 * lines] = near_matrix
    gather[:lines] = one_hot(iota((lines, rows), 1) == near_col)
    gain[...] = jnp.broadcast_to(to_column(line_gain[...], lines), (lines, width))
    on = switch_on[...].astype(F32) * switch_cond[...]
    eight = jnp.concatenate([on, jnp.zeros((8 - steps, rows), F32)], axis=0)
    columns = eight.T
    for step in range(steps):
        switched[step] = jnp.broadcast_to(columns[:, step : step + 1], (rows, width))
    for load in loads[1:]:
        load.wait()

    wait_subs(ra0, 0)
    ob0[...] = turn(ra0[...])
    send_zones(ob0, rb0, 0)
    wait_subs(ra1, 1)
    ob1[...] = turn(ra1[...])
    send_zones(ob1, rb1, 1)

    wait_zones(rb0, 0)
    arrived = rb0[:, :, half:].reshape(slots, 128)

    def node_of(numbers):
        numbers = numbers.astype(F32)
        return numbers[:, 0:1] * 16.0 + numbers[:, 64:65] - 1.0

    scatter[:, 2 * lines :] = one_hot(
        iota((rows, slots), 0) == to_row(node_of(arrived), slots).astype(jnp.int32)
    )
    gather[lines:] = one_hot(iota((slots, rows), 1) == node_of(dot(swap[...], arrived)).astype(jnp.int32))

    def set_near(history):
        top = history.astype(BF16)
        rhs[:lines] = top
        rhs[lines : 2 * lines] = (history - top.astype(F32)).astype(BF16)

    def inject(step, g, volts):
        at = pl.ds(pl.multiple_of(g * width, width), width)
        faulted = me * rows + iota((rows, width), 0) == fault_node[:, at]
        conduct = switched[step] + jnp.where(faulted, fault_cond[:, at], 0.0)
        lines_in = dot(scatter[...], rhs[...])
        x[step, g, :rows] = (src[step, :, at].astype(F32) + lines_in - conduct * volts).astype(BF16)
        for peer, place, sem in ((right, 1, left_sem), (left, 2, right_sem)):
            own_copy(step, g, peer, place, sem).start()

    def own_copy(step, g, peer, place, sem):
        return pltpu.make_async_remote_copy(
            src_ref=x.at[step, g, pl.ds(0, rows)],
            dst_ref=x.at[step, g, pl.ds(place * rows, rows)],
            send_sem=send_sem.at[step, g],
            recv_sem=sem.at[step, g],
            device_id={"row": peer},
            device_id_type=MESH,
        )

    def pass_on(step, g, peer, place, offset):
        return pltpu.make_async_remote_copy(
            src_ref=x.at[step, g, pl.ds(place * rows + offset, rows // 2)],
            dst_ref=x.at[step, g, pl.ds(3 * rows + offset, rows // 2)],
            send_sem=send_sem.at[step, g],
            recv_sem=far_sem.at[step, g],
            device_id={"row": peer},
            device_id_type=MESH,
        )

    def whole(step, g, count, sem):
        part = x.at[step, g, pl.ds(0, count * rows)]
        return pltpu.make_async_remote_copy(
            src_ref=part,
            dst_ref=part,
            send_sem=send_sem.at[step, g],
            recv_sem=sem.at[step, g],
            device_id={"row": right},
            device_id_type=MESH,
        )

    for g in range(GROUPS):
        if g == 2:
            wait_zones(rb1, 1)
        set_near(hist_near[0, :, g * width : (g + 1) * width])
        got = rb0 if g < 2 else rb1
        rhs[2 * lines :] = got[:, :, (g % 2) * width : (g % 2 + 1) * width].reshape(slots, width)
        inject(0, g, v[g])

    wait_subs(ra2, 2)
    ob2[...] = turn(ra2[...])
    send_zones(ob2, rb2, 2)

    def begin(item):
        step, g = item // GROUPS, lax.rem(item, GROUPS)
        whole(step, g, 1, left_sem).wait_recv()
        pass_on(step, g, right, 1, 0).start()
        whole(step, g, 1, right_sem).wait_recv()
        pass_on(step, g, left, 2, rows // 2).start()
        v[g] = dot(zr[:, : 3 * rows], x[step, g, : 3 * rows])

    def finish(item):
        step, g = item // GROUPS, lax.rem(item, GROUPS)
        pair, side = g // 2, lax.rem(g, 2)
        at = pl.ds(pl.multiple_of(g * width, width), width)
        in_half = pl.ds(pl.multiple_of(side * width, width), width)
        whole(step, g, 1, far_sem).wait_recv()
        v[g] += dot(zr[:, 3 * rows :], x[step, g, 3 * rows :])

        @pl.when(step == 0)
        def _():
            @pl.when(g == 0)
            def _():
                wait_zones(rb2, 2)

            set_near(hist_near[1, :, at])
            rhs[2 * lines :] = rb2[:, :, at].reshape(slots, width)

        @pl.when((step == 1) | (step == 2))
        def _():
            which = (step - 1) * 2 + pair

            @pl.when(side == 0)
            def _():
                wait_zones(rb.at[which], 3 + which)

            rhs[2 * lines :] = rb[which, :, :block_b, in_half].reshape(slots, width)
            returned = rb[which, :, block_b:, in_half].reshape(slots, width)
            set_near(gain[...] * dot(slots_back[...], returned) - hist_far[step - 1, :, at])

        @pl.when(step < steps - 1)
        def _():
            inject(step + 1, g, v[g])

        @pl.when(step == steps - 1)
        def _():
            pltpu.make_async_copy(v.at[g], out_hbm.at[:, at], out_sem.at[g]).start()

        @pl.when(step < 2)
        def _():
            which = step * 2 + pair
            volts = v[g]
            top = volts.astype(BF16)
            ends = dot(gather[...], top)
            near_volts = ends[:lines] + dot(gather[:lines], (volts - top.astype(F32)).astype(BF16))
            history = gain[...] * near_volts - hist_near[step, :, at]
            oa[which, :, :block_a, in_half] = (
                dot(slots_out[...], history.astype(BF16)).astype(BF16).reshape(subs, block_a, width)
            )
            oa[which, :, block_a:, in_half] = ends[lines:].astype(BF16).reshape(subs, block_a, width)

            @pl.when(side == 1)
            def _():
                send_subs(oa.at[which], ra.at[which], 3 + which)

        @pl.when((side == 0) & (item >= 2) & (item < 2 + 4 * 2))
        def _():
            which = item // 2 - 1
            wait_subs(ra.at[which], 3 + which)
            ob[which, :, :block_b] = turn(ra[which, :, :block_a])
            ob[which, :, block_b:] = turn(ra[which, :, block_a:])
            send_zones(ob.at[which], rb.at[which], 3 + which)

    for item in range(AHEAD):
        begin(item)

    def body(item, carry):
        @pl.when(item + AHEAD < items)
        def _():
            begin(item + AHEAD)

        finish(item)

        @pl.when(item >= GROUPS)
        def _():
            whole(item // GROUPS - 1, lax.rem(item, GROUPS), 3, far_sem).wait_send()

        return carry

    lax.fori_loop(0, items, body, 0)

    for g in range(GROUPS):
        whole(steps - 1, g, 3, far_sem).wait_send()
    for which, (sent_a, sent_b) in enumerate(((oa0, ob0), (oa1, ob1), (oa2, ob2))):
        all_of(sent_a, which, 0, "sub", subs).wait_send()
        all_of(sent_b, which, 1, "zone", zones).wait_send()
    for which in range(4):
        all_of(oa.at[which], 3 + which, 0, "sub", subs).wait_send()
        all_of(ob.at[which], 3 + which, 1, "zone", zones).wait_send()
    for g in range(GROUPS):
        at = pl.ds(g * width, width)
        pltpu.make_async_copy(v.at[g], out_hbm.at[:, at], out_sem.at[g]).wait()


def local(zones, subs, *arguments):
    (
        z_inverse,
        sources,
        v_start,
        hist_near,
        hist_far,
        switch_on,
        switch_cond,
        fault_node,
        fault_cond,
        remote_sub,
        near_node,
        far_node,
        line_gain,
    ) = arguments
    steps, _, rows, cases = sources.shape
    lines = near_node.shape[1]
    slots = 2 * zones * subs
    block_a, block_b = 2 * zones, 2 * subs
    width = cases // GROUPS
    half = 2 * width

    def exchange(wide, tall=1, count=None):
        lead = () if count is None else (count,)
        return [
            pltpu.VMEM(lead + (subs, tall * block_a, wide), BF16),
            pltpu.VMEM(lead + (subs, tall * block_a, wide), BF16),
            pltpu.VMEM(lead + (zones, tall * block_b, wide), BF16),
            pltpu.VMEM(lead + (zones, tall * block_b, wide), BF16),
        ]

    hbm = pl.BlockSpec(memory_space=pl.ANY)
    vmem = pl.BlockSpec(memory_space=pltpu.VMEM)
    result = pl.pallas_call(
        functools.partial(kernel, zones, subs),
        out_shape=jax.ShapeDtypeStruct((rows, cases), F32),
        in_specs=[hbm] * 5 + [vmem] * 8,
        out_specs=hbm,
        scratch_shapes=[
            pltpu.VMEM((rows, 4 * rows), BF16),
            pltpu.VMEM((steps, GROUPS, 4 * rows, width), BF16),
            pltpu.VMEM((GROUPS, rows, width), F32),
            pltpu.VMEM((steps, rows, cases), BF16),
            pltpu.VMEM((2, lines, cases), F32),
            pltpu.VMEM((2, lines, cases), F32),
            pltpu.VMEM((steps, rows, width), F32),
            pltpu.VMEM((rows, 2 * lines + slots), BF16),
            pltpu.VMEM((lines + slots, rows), BF16),
            pltpu.VMEM((slots, lines), BF16),
            pltpu.VMEM((lines, slots), BF16),
            pltpu.VMEM((slots, slots), BF16),
            pltpu.VMEM((lines, width), F32),
            pltpu.VMEM((2 * lines + slots, width), BF16),
            *exchange(half + 128),
            *exchange(half),
            *exchange(cases),
            *exchange(half, 2, 4),
            pltpu.SemaphoreType.DMA((3 + GROUPS + 4,)),
            pltpu.SemaphoreType.DMA((steps, GROUPS)),
            pltpu.SemaphoreType.DMA((steps, GROUPS)),
            pltpu.SemaphoreType.DMA((steps, GROUPS)),
            pltpu.SemaphoreType.DMA((steps, GROUPS)),
            pltpu.SemaphoreType.DMA((7, 2)),
            pltpu.SemaphoreType.DMA((7, 2)),
            pltpu.SemaphoreType.DMA((GROUPS,)),
        ],
        compiler_params=pltpu.CompilerParams(
            collective_id=0, has_side_effects=True, vmem_limit_bytes=40 * 1024 * 1024
        ),
    )(
        z_inverse[0],
        sources[:, 0],
        v_start[0],
        hist_near[:, 0],
        hist_far[:, 0],
        switch_on[:, 0],
        switch_cond,
        fault_node[None],
        fault_cond[None],
        remote_sub[:, :, 0],
        near_node,
        far_node,
        line_gain,
    )
    return result[None]


def solution(mesh):
    placed = (
        P(("zone", "sub"), "row", None),
        P(None, ("zone", "sub"), "row", None),
        P(("zone", "sub"), "row", None),
        P(None, ("zone", "sub"), "row", None),
        P(None, ("zone", "sub"), "row", None),
        P(None, ("zone", "sub"), "row"),
        P(("zone", "sub"), "row"),
        P(),
        P(),
        P(("zone", "sub"), "row", None),
        P(("zone", "sub"), "row"),
        P(("zone", "sub"), "row"),
        P(("zone", "sub"), "row"),
    )
    return jax.shard_map(
        functools.partial(local, mesh.shape["zone"], mesh.shape["sub"]),
        mesh=mesh,
        in_specs=placed,
        out_specs=P(("zone", "sub"), "row", None),
        check_vma=False,
    )
```

time: 276 us -> 107 us (0.39)
  Pallas kernels: 0 us -> 93.3 us
  waiting for transfers between devices: 64.8 us -> 0 us
  blocking collectives: 60 us -> 0 us
  other arithmetic: 39.2 us -> 0 us
  starting transfers between devices: 38.2 us -> 0 us
  local copies, waits for them, and re-layouts: 42.1 us -> 12.6 us
  matrix products: 14.8 us -> 0 us
  between operations: 13.4 us -> 0.02 us
    pallas_call x0 -> x1, Pallas kernels: none -> 93.3 us  [local(): pl.pallas_call(functools.partial(kernel, zones, subs), out_shape=jax.Shap...]
    all_to_all x3 -> x0, blocking collectives: 60 us -> none  [send_lines(): lax.all_to_all(buffer, ('zone', 'sub'), split_axis=0, concat_axis=0, tile...]
    all_gather x4 -> x0, waiting for transfers between devices: 48.2 us -> none  [local(): lax.all_gather(injb, 'row', axis=0, tiled=True)]
    all_to_all x4 -> x0, starting transfers between devices: 38 us -> none  [the longest x3 25.8 us: send_lines(): lax.all_to_all(buffer, ('zone', 'sub'), split_axis=0, concat_axis=0, tile...]
    all_to_all x4 -> x0, waiting for transfers between devices: 16.5 us -> none  [the longest x3 15.5 us: send_lines(): lax.all_to_all(buffer, ('zone', 'sub'), split_axis=0, concat_axis=0, tile...]
    all_to_all x13 -> x0, local copies, waits for them, and re-layouts: 16.3 us -> none  [the longest x10 13.5 us: send_lines(): lax.all_to_all(buffer, ('zone', 'sub'), split_axis=0, concat_axis=0, tile...]
    scatter-add x4 -> x0, other arithmetic: 15.2 us -> none  [local(): jnp.zeros((rows, cases), jnp.float32).at[all_index].add(values, mode='drop')]
    dot_general x4 -> x0, matrix products: 14.8 us -> none  [local(): jnp.dot(inverse_rows, lax.all_gather(injb, 'row', axis=0, tiled=True), pr...]
  transfers between devices with their start and end apart: 8 -> 0, of which waited for: 7 -> 0; matrix products, arithmetic and copies ran while one was open for 16% -> 0% of each run, Pallas kernels for 0% -> 0%
where the time goes in v1:
time: 107 us; the launch traced here: 106 us
  Pallas kernels  93.3 us (87%)
  local copies, waits for them, and re-layouts  12.6 us (12%)
    pallas_call x1, Pallas kernels, local(): pl.pallas_call(functools.partial(kernel, zones, subs), out_shape=jax.Shap...  93.3 us
    unnamed x26, local copies, waits for them, and re-layouts  12.6 us

profile of v1, /device:TPU:8, one launch (start us, length us, event | category | flops | bytes accessed | tf_op | source)
XLA Modules:
  0.0 105.9 jit_solution(13270885368527429951)
XLA Ops:
  0.0 0.7 copy.16
  0.7 0.0 copy-start
  0.7 1.6 %copy-done = bf16[1,512,2048]{2,1,0:T(8,128)(2,1)S(1)} copy-done((bf16[1,512,2048]{2,1,0:T(8,128)(2,1)S(1)}, bf16[1,512,2048]{2,1,0:T(8,128)(2,1)}, u32[]{:S(2)}) %copy-start) | copy-done | bytes 2097176
  2.3 0.0 copy-start.1
  2.3 1.6 %copy-done.1 = bf16[4,1,512,512]{3,2,1,0:T(8,128)(2,1)S(1)} copy-done((bf16[4,1,512,512]{3,2,1,0:T(8,128)(2,1)S(1)}, bf16[4,1,512,512]{3,2,1,0:T(8,128)(2,1)}, u32[]{:S(2)}) %copy-start.1) | copy-done | bytes 2097176
  3.9 0.0 copy-start.2
  3.9 1.2 %copy-done.2 = f32[1,512,512]{2,1,0:T(8,128)S(1)} copy-done((f32[1,512,512]{2,1,0:T(8,128)S(1)}, f32[1,512,512]{2,1,0:T(8,128)}, u32[]{:S(2)}) %copy-start.2) | copy-done | bytes 1048600
  5.1 0.0 copy-start.3
  5.1 0.9 copy-done.3
  6.1 0.0 copy-start.4
  6.1 0.9 copy-done.4
  7.0 0.0 copy-start.5
  7.0 0.7 copy-done.5
  7.7 0.0 copy-start.6
  7.7 0.7 copy-done.6
  8.4 0.0 copy-start.7
  8.4 0.7 copy-done.7
  9.1 0.0 copy-start.8
  9.1 0.7 copy-done.8
  9.7 0.0 copy-start.9
  9.7 0.7 copy-done.9
  10.4 0.0 copy-start.10
  10.4 0.7 copy-done.10
  11.0 0.0 copy-start.11
  11.0 0.7 copy-done.11
  11.7 93.3 %shard_map.127 = f32[512,512]{1,0:T(8,128)S(1)} custom-call(bf16[512,2048]{1,0:T(8,128)(2,1)S(1)} %bitcast.13, bf16[4,512,512]{2,1,0:T(8,128)(2,1)S(1)} %bitcast.14, f32[512,512]{1,0:T(8,128)S(1)} %bitcast.15, f32[2,64,512]{2,1,0:T(8,128)S(1)} %bitcast.16, f32[2,64,512]{2,1,0:T(8,128)S(1)} %bitcast.17, s32[4,512]{1,0:T(4,128)S(1)} %bitcast.18, ...), custom_call_target="tpu_custom_call" | custom-call | tf_op jit(solution)/shard_map/pallas_call | solution.py:450
  104.9 1.0 copy.18
Async XLA Ops:
  0.7 1.6 %copy-start = (bf16[1,512,2048]{2,1,0:T(8,128)(2,1)S(1)}, bf16[1,512,2048]{2,1,0:T(8,128)(2,1)}, u32[]{:S(2)}) copy-start(bf16[1,512,2048]{2,1,0:T(8,128)(2,1)} %param.13) | copy-start | bytes 6291460
  2.3 1.6 %copy-start.1 = (bf16[4,1,512,512]{3,2,1,0:T(8,128)(2,1)S(1)}, bf16[4,1,512,512]{3,2,1,0:T(8,128)(2,1)}, u32[]{:S(2)}) copy-start(bf16[4,1,512,512]{3,2,1,0:T(8,128)(2,1)} %param.14) | copy-start | bytes 6291460
  3.9 1.2 %copy-start.2 = (f32[1,512,512]{2,1,0:T(8,128)S(1)}, f32[1,512,512]{2,1,0:T(8,128)}, u32[]{:S(2)}) copy-start(f32[1,512,512]{2,1,0:T(8,128)} %param.15) | copy-start | bytes 3145732
  5.1 0.9 copy-start.3
  6.1 0.9 copy-start.4
  7.0 0.7 copy-start.5
  7.7 0.7 copy-start.6
  8.4 0.7 copy-start.7
  9.1 0.7 copy-start.8
  9.7 0.7 copy-start.9
  10.4 0.7 copy-start.10
  11.0 0.7 copy-start.11

commit v2 on v1

--- a/solution.py
+++ b/solution.py
@@ -11,7 +11,7 @@
 F32 = jnp.float32
 BF16 = jnp.bfloat16
 GROUPS = 4
-AHEAD = 1
+AHEAD = 2
 
 
 def dot(a, b):
@@ -44,54 +44,59 @@
     vs_hbm,
     near_hbm,
     far_hbm,
-    switch_on,
-    switch_cond,
-    fault_node,
-    fault_cond,
-    remote_sub,
-    near_node,
-    far_node,
-    line_gain,
-    out_hbm,
-    zr,
-    x,
-    v,
-    src,
-    hist_near,
-    hist_far,
-    switched,
-    scatter,
-    gather,
-    slots_out,
-    slots_back,
-    swap,
-    gain,
-    rhs,
-    oa0,
-    ra0,
-    ob0,
-    rb0,
-    oa1,
-    ra1,
-    ob1,
-    rb1,
-    oa2,
-    ra2,
-    ob2,
-    rb2,
-    oa,
-    ra,
-    ob,
-    rb,
-    load_sem,
-    send_sem,
-    left_sem,
-    right_sem,
-    far_sem,
-    ex_send,
-    ex_recv,
-    out_sem,
+    *rest,
 ):
+    small_hbm, out_hbm, small, rest = rest[:8], rest[8], rest[9:17], rest[17:]
+    (
+        switch_on,
+        switch_cond,
+        fault_node,
+        fault_cond,
+        remote_sub,
+        near_node,
+        far_node,
+        line_gain,
+    ) = small
+    (
+        zr,
+        x,
+        v,
+        src,
+        hist_near,
+        hist_far,
+        switched,
+        scatter,
+        gather,
+        slots_out,
+        slots_back,
+        swap,
+        gain,
+        rhs,
+        oa0,
+        ra0,
+        ob0,
+        rb0,
+        oa1,
+        ra1,
+        ob1,
+        rb1,
+        oa2,
+        ra2,
+        ob2,
+        rb2,
+        oa,
+        ra,
+        ob,
+        rb,
+        load_sem,
+        send_sem,
+        left_sem,
+        right_sem,
+        far_sem,
+        ex_send,
+        ex_recv,
+        out_sem,
+    ) = rest
     rows, nodes = z_hbm.shape
     steps, _, cases = src_hbm.shape
     lines = near_node.shape[1]
@@ -103,7 +108,11 @@
     my_zone, my_sub, me = (lax.axis_index(name) for name in ("zone", "sub", "row"))
     right, left, across = lax.rem(me + 1, 4), lax.rem(me + 3, 4), lax.rem(me + 2, 4)
 
-    loads = [pltpu.make_async_copy(far_hbm, hist_far, load_sem.at[0])]
+    loads = [
+        pltpu.make_async_copy(there, here, load_sem.at[3 + GROUPS + 4 + number])
+        for number, (there, here) in enumerate(zip(small_hbm, small))
+    ]
+    loads.append(pltpu.make_async_copy(far_hbm, hist_far, load_sem.at[0]))
     loads.append(pltpu.make_async_copy(near_hbm, hist_near, load_sem.at[1]))
     loads.append(pltpu.make_async_copy(src_hbm, src, load_sem.at[2]))
     for g in range(GROUPS):
@@ -127,6 +136,9 @@
         pl.semaphore_signal(barrier, inc=1, device_id={"sub": lax.rem(my_sub + d, subs)}, device_id_type=MESH)
     for d in range(1, zones):
         pl.semaphore_signal(barrier, inc=1, device_id={"zone": lax.rem(my_zone + d, zones)}, device_id_type=MESH)
+
+    for load in loads[:8]:
+        load.wait()
 
     target = remote_sub[...].astype(F32)
     target_col = to_column(target, lines)
@@ -204,7 +216,7 @@
         values = got.reshape(slots, got.shape[-1])
         return dot(swap[...], values).astype(BF16).reshape(zones, block_b, got.shape[-1])
 
-    loads[0].wait()
+    loads[8].wait()
     spread = slots_out[...]
     for step in range(2):
         values = dot(spread, hist_far[step].astype(BF16)).astype(BF16)
@@ -228,12 +240,12 @@
     scatter[:, lines : 2 * lines] = near_matrix
     gather[:lines] = one_hot(iota((lines, rows), 1) == near_col)
     gain[...] = jnp.broadcast_to(to_column(line_gain[...], lines), (lines, width))
-    on = switch_on[...].astype(F32) * switch_cond[...]
+    on = switch_on[:, 0].astype(F32) * switch_cond[...]
     eight = jnp.concatenate([on, jnp.zeros((8 - steps, rows), F32)], axis=0)
     columns = eight.T
     for step in range(steps):
         switched[step] = jnp.broadcast_to(columns[:, step : step + 1], (rows, width))
-    for load in loads[1:]:
+    for load in loads[9:]:
         load.wait()
 
     wait_subs(ra0, 0)
@@ -445,14 +457,24 @@
             pltpu.VMEM(lead + (zones, tall * block_b, wide), BF16),
         ]
 
-    hbm = pl.BlockSpec(memory_space=pl.ANY)
-    vmem = pl.BlockSpec(memory_space=pltpu.VMEM)
+    hbm = pl.BlockSpec(memory_space=pltpu.HBM)
+    small = (
+        switch_on,
+        switch_cond,
+        fault_node[None],
+        fault_cond[None],
+        remote_sub[:, :, 0],
+        near_node,
+        far_node,
+        line_gain,
+    )
     result = pl.pallas_call(
         functools.partial(kernel, zones, subs),
         out_shape=jax.ShapeDtypeStruct((rows, cases), F32),
-        in_specs=[hbm] * 5 + [vmem] * 8,
+        in_specs=[hbm] * (5 + len(small)),
         out_specs=hbm,
         scratch_shapes=[
+            *(pltpu.VMEM(array.shape, array.dtype) for array in small),
             pltpu.VMEM((rows, 4 * rows), BF16),
             pltpu.VMEM((steps, GROUPS, 4 * rows, width), BF16),
             pltpu.VMEM((GROUPS, rows, width), F32),
@@ -471,7 +493,7 @@
             *exchange(half),
             *exchange(cases),
             *exchange(half, 2, 4),
-            pltpu.SemaphoreType.DMA((3 + GROUPS + 4,)),
+            pltpu.SemaphoreType.DMA((3 + GROUPS + 4 + 8,)),
             pltpu.SemaphoreType.DMA((steps, GROUPS)),
             pltpu.SemaphoreType.DMA((steps, GROUPS)),
             pltpu.SemaphoreType.DMA((steps, GROUPS)),
@@ -481,7 +503,7 @@
             pltpu.SemaphoreType.DMA((GROUPS,)),
         ],
         compiler_params=pltpu.CompilerParams(
-            collective_id=0, has_side_effects=True, vmem_limit_bytes=40 * 1024 * 1024
+            collective_id=0, has_side_effects=True, vmem_limit_bytes=56 * 1024 * 1024
         ),
     )(
         z_inverse[0],
@@ -489,14 +511,7 @@
         v_start[0],
         hist_near[:, 0],
         hist_far[:, 0],
-        switch_on[:, 0],
-        switch_cond,
-        fault_node[None],
-        fault_cond[None],
-        remote_sub[:, :, 0],
-        near_node,
-        far_node,
-        line_gain,
+        *small,
     )
     return result[None]
 

time: 107 us -> 94.9 us (0.89)
  local copies, waits for them, and re-layouts: 12.6 us -> 2.26 us
    unnamed x26 -> x1, local copies, waits for them, and re-layouts: 12.6 us -> 2.26 us
where the time goes in v2:
time: 94.9 us; the launch traced here: 94.7 us
  Pallas kernels  92.5 us (97%)
  local copies, waits for them, and re-layouts  2.26 us (2%)
    pallas_call x1, Pallas kernels, local(): pl.pallas_call(functools.partial(kernel, zones, subs), out_shape=jax.Shap...  92.5 us
    unnamed x1, local copies, waits for them, and re-layouts  2.26 us

profile of v2, /device:TPU:8, one launch (start us, length us, event | category | flops | bytes accessed | tf_op | source)
XLA Modules:
  0.0 94.7 jit_solution(14128848063485861878)
XLA Ops:
  0.0 92.5 %shard_map.127 = f32[512,512]{1,0:T(8,128)} custom-call(bf16[512,2048]{1,0:T(8,128)(2,1)} %bitcast.10, bf16[4,512,512]{2,1,0:T(8,128)(2,1)} %bitcast.11, f32[512,512]{1,0:T(8,128)} %bitcast.12, f32[2,64,512]{2,1,0:T(8,128)} %bitcast.13, f32[2,64,512]{2,1,0:T(8,128)} %bitcast.14, s32[4,1,512]{2,1,0:T(1,128)} %rest_0_.1, f32[1,512]{1,0:T(1,128)} %rest_1_.1, ...), custom_call_target="tpu_custom_call" | custom-call | tf_op jit(solution)/shard_map/pallas_call | solution.py:471
  92.5 2.3 %copy.15 = f32[1,512,512]{2,1,0:T(8,128)} copy(f32[1,512,512]{2,1,0:T(8,128)} %bitcast.9) | data formatting | bytes 2097152

commit v3 on v2

--- a/solution.py
+++ b/solution.py
@@ -11,6 +11,7 @@
 F32 = jnp.float32
 BF16 = jnp.bfloat16
 GROUPS = 4
+EARLY = 2
 AHEAD = 2
 
 
@@ -88,6 +89,10 @@
         ra,
         ob,
         rb,
+        late_lines,
+        selected,
+        fix_send,
+        fix_recv,
         load_sem,
         send_sem,
         left_sem,
@@ -101,9 +106,10 @@
     steps, _, cases = src_hbm.shape
     lines = near_node.shape[1]
     slots = 2 * zones * subs
-    block_a, block_b = 2 * zones, 2 * subs
+    block_a, block_b = 2 * subs, 2 * zones
     width = cases // GROUPS
     half = 2 * width
+    early, late = EARLY * width, (GROUPS - EARLY) * width
     items = steps * GROUPS
     my_zone, my_sub, me = (lax.axis_index(name) for name in ("zone", "sub", "row"))
     right, left, across = lax.rem(me + 1, 4), lax.rem(me + 3, 4), lax.rem(me + 2, 4)
@@ -147,91 +153,55 @@
     rank = jnp.sum(jnp.where(same & (first < second), 1.0, 0.0), axis=0, keepdims=True)
     rank_col = jnp.sum(jnp.where(same & (second < first), 1.0, 0.0), axis=1, keepdims=True)
     target_int = remote_sub[...]
-    zone_of = target_int // subs
-    sub_of = target_int - zone_of * subs
-    slot_a = sub_of * block_a + zone_of * 2 + rank.astype(jnp.int32)
-    slot_b = (target_col * 2.0 + rank_col).astype(jnp.int32)
+    slot_a = target_int * 2 + rank.astype(jnp.int32)
+    zone_col = target_col.astype(jnp.int32) // subs
+    sub_col = target_col.astype(jnp.int32) - zone_col * subs
+    slot_b = sub_col * block_b + zone_col * 2 + rank_col.astype(jnp.int32)
     slots_out[...] = one_hot(iota((slots, lines), 0) == slot_a)
     slots_back[...] = one_hot(iota((lines, slots), 1) == slot_b)
     k = iota((slots, slots), 0)
-    z_of, rest = k // (2 * subs), k - (k // (2 * subs)) * (2 * subs)
-    swap[...] = one_hot(iota((slots, slots), 1) == (rest // 2) * block_a + z_of * 2 + (rest - (rest // 2) * 2))
+    sub_of, rest = k // block_b, k - (k // block_b) * block_b
+    swap[...] = one_hot(iota((slots, slots), 1) == (rest // 2) * block_a + sub_of * 2 + (rest - (rest // 2) * 2))
     far_col = (to_column(far_node[...].astype(F32), lines) + 1.0).astype(jnp.int32)
     high = far_col // 16
     numbers = jnp.where(iota((lines, 128), 1) < 64, high, far_col - high * 16).astype(F32).astype(BF16)
     numbers_out = dot(slots_out[...], numbers).astype(BF16)
 
-    def send_subs(out, got, which):
-        got[pl.ds(my_sub, 1)] = out[pl.ds(my_sub, 1)]
+    hops = (("zone", my_zone, zones), ("sub", my_sub, subs))
+
+    def send_hop(phase, out, got, which):
+        axis, my, size = hops[phase]
+        got[pl.ds(my, 1)] = out[pl.ds(my, 1)]
 
         def one(d, carry):
-            partner = lax.rem(my_sub + d, subs)
+            partner = lax.rem(my + d, size)
             pltpu.make_async_remote_copy(
                 src_ref=out.at[partner],
-                dst_ref=got.at[my_sub],
-                send_sem=ex_send.at[which, 0],
-                recv_sem=ex_recv.at[which, 0],
-                device_id={"sub": partner},
+                dst_ref=got.at[my],
+                send_sem=ex_send.at[which, phase],
+                recv_sem=ex_recv.at[which, phase],
+                device_id={axis: partner},
                 device_id_type=MESH,
             ).start()
             return carry
 
-        lax.fori_loop(1, subs, one, 0)
-
-    def send_zones(out, got, which):
-        got[pl.ds(my_zone, 1)] = out[pl.ds(my_zone, 1)]
-
-        def one(d, carry):
-            partner = lax.rem(my_zone + d, zones)
-            pltpu.make_async_remote_copy(
-                src_ref=out.at[partner],
-                dst_ref=got.at[my_zone],
-                send_sem=ex_send.at[which, 1],
-                recv_sem=ex_recv.at[which, 1],
-                device_id={"zone": partner},
-                device_id_type=MESH,
-            ).start()
-            return carry
-
-        lax.fori_loop(1, zones, one, 0)
-
-    def all_of(buffer, which, phase, axis, size):
+        lax.fori_loop(1, size, one, 0)
+
+    def all_of(phase, buffer, which):
+        axis, my, size = hops[phase]
         part = buffer.at[pl.ds(0, size - 1)]
         return pltpu.make_async_remote_copy(
             src_ref=part,
             dst_ref=part,
             send_sem=ex_send.at[which, phase],
             recv_sem=ex_recv.at[which, phase],
-            device_id={axis: 0},
+            device_id={axis: lax.rem(my + 1, size)},
             device_id_type=MESH,
         )
-
-    def wait_subs(buffer, which):
-        all_of(buffer, which, 0, "sub", subs).wait_recv()
-
-    def wait_zones(buffer, which):
-        all_of(buffer, which, 1, "zone", zones).wait_recv()
 
     def turn(got):
         values = got.reshape(slots, got.shape[-1])
-        return dot(swap[...], values).astype(BF16).reshape(zones, block_b, got.shape[-1])
-
-    loads[8].wait()
-    spread = slots_out[...]
-    for step in range(2):
-        values = dot(spread, hist_far[step].astype(BF16)).astype(BF16)
-        if step == 0:
-            oa0[:, :, :half] = values[:, :half].reshape(subs, block_a, half)
-            oa0[:, :, half:] = numbers_out.reshape(subs, block_a, 128)
-            oa1[...] = values[:, half:].reshape(subs, block_a, half)
-        else:
-            oa2[...] = values.reshape(subs, block_a, cases)
-        if step == 0:
-            pl.semaphore_wait(barrier, 2 + subs - 1 + zones - 1)
-            send_subs(oa0, ra0, 0)
-            send_subs(oa1, ra1, 1)
-        else:
-            send_subs(oa2, ra2, 2)
+        return dot(swap[...], values).astype(BF16).reshape(subs, block_b, got.shape[-1])
 
     near_row = near_node[...]
     near_col = to_column(near_row.astype(F32), lines).astype(jnp.int32)
@@ -245,39 +215,27 @@
     columns = eight.T
     for step in range(steps):
         switched[step] = jnp.broadcast_to(columns[:, step : step + 1], (rows, width))
-    for load in loads[9:]:
-        load.wait()
-
-    wait_subs(ra0, 0)
-    ob0[...] = turn(ra0[...])
-    send_zones(ob0, rb0, 0)
-    wait_subs(ra1, 1)
-    ob1[...] = turn(ra1[...])
-    send_zones(ob1, rb1, 1)
-
-    wait_zones(rb0, 0)
-    arrived = rb0[:, :, half:].reshape(slots, 128)
-
-    def node_of(numbers):
-        numbers = numbers.astype(F32)
-        return numbers[:, 0:1] * 16.0 + numbers[:, 64:65] - 1.0
-
-    scatter[:, 2 * lines :] = one_hot(
-        iota((rows, slots), 0) == to_row(node_of(arrived), slots).astype(jnp.int32)
-    )
-    gather[lines:] = one_hot(iota((slots, rows), 1) == node_of(dot(swap[...], arrived)).astype(jnp.int32))
+
+    loads[8].wait()
+    spread = slots_out[...]
+    values = dot(spread, hist_far[0].astype(BF16)).astype(BF16)
+    oa0[:, :, :early] = values[:, :early].reshape(zones, block_a, early)
+    oa0[:, :, early:] = numbers_out.reshape(zones, block_a, 128)
+    oa1[...] = values[:, early:].reshape(zones, block_a, late)
+    oa2[...] = dot(spread, hist_far[1].astype(BF16)).astype(BF16).reshape(zones, block_a, cases)
 
     def set_near(history):
         top = history.astype(BF16)
         rhs[:lines] = top
         rhs[lines : 2 * lines] = (history - top.astype(F32)).astype(BF16)
 
-    def inject(step, g, volts):
+    def inject(step, g, volts, lines_in):
         at = pl.ds(pl.multiple_of(g * width, width), width)
         faulted = me * rows + iota((rows, width), 0) == fault_node[:, at]
         conduct = switched[step] + jnp.where(faulted, fault_cond[:, at], 0.0)
-        lines_in = dot(scatter[...], rhs[...])
         x[step, g, :rows] = (src[step, :, at].astype(F32) + lines_in - conduct * volts).astype(BF16)
+
+    def send_own(step, g):
         for peer, place, sem in ((right, 1, left_sem), (left, 2, right_sem)):
             own_copy(step, g, peer, place, sem).start()
 
@@ -312,39 +270,120 @@
             device_id_type=MESH,
         )
 
-    for g in range(GROUPS):
-        if g == 2:
-            wait_zones(rb1, 1)
-        set_near(hist_near[0, :, g * width : (g + 1) * width])
-        got = rb0 if g < 2 else rb1
-        rhs[2 * lines :] = got[:, :, (g % 2) * width : (g % 2 + 1) * width].reshape(slots, width)
-        inject(0, g, v[g])
-
-    wait_subs(ra2, 2)
-    ob2[...] = turn(ra2[...])
-    send_zones(ob2, rb2, 2)
-
     def begin(item):
         step, g = item // GROUPS, lax.rem(item, GROUPS)
         whole(step, g, 1, left_sem).wait_recv()
         pass_on(step, g, right, 1, 0).start()
         whole(step, g, 1, right_sem).wait_recv()
         pass_on(step, g, left, 2, rows // 2).start()
-        v[g] = dot(zr[:, : 3 * rows], x[step, g, : 3 * rows])
+
+    def correct(peer, place, sem):
+        return pltpu.make_async_remote_copy(
+            src_ref=late_lines.at[0],
+            dst_ref=late_lines.at[place],
+            send_sem=fix_send.at[place - 1],
+            recv_sem=sem,
+            device_id={"row": peer},
+            device_id_type=MESH,
+        )
+
+    def correct_on(peer, place, offset):
+        return pltpu.make_async_remote_copy(
+            src_ref=late_lines.at[place, pl.ds(offset, slots // 2)],
+            dst_ref=late_lines.at[3, pl.ds(offset, slots // 2)],
+            send_sem=fix_send.at[place + 1],
+            recv_sem=fix_recv.at[place + 1],
+            device_id={"row": peer},
+            device_id_type=MESH,
+        )
+
+    corrections = (correct(right, 1, fix_recv.at[0]), correct(left, 2, fix_recv.at[1]))
+    corrections_on = (correct_on(right, 1, 0), correct_on(left, 2, slots // 2))
+
+    for load in loads[9:]:
+        load.wait()
+    for g in range(EARLY):
+        set_near(hist_near[0, :, g * width : (g + 1) * width])
+        inject(0, g, v[g], dot(scatter[:, : 2 * lines], rhs[: 2 * lines]))
+    pl.semaphore_wait(barrier, 2 + subs - 1 + zones - 1)
+    send_hop(0, oa0, ra0, 0)
+    for g in range(2):
+        send_own(0, g)
+    send_hop(0, oa1, ra1, 1)
+    send_hop(0, oa2, ra2, 2)
+    for which, (got, out, last) in enumerate(((ra0, ob0, rb0), (ra1, ob1, rb1))):
+        all_of(0, got, which).wait_recv()
+        out[...] = turn(got[...])
+        send_hop(1, out, last, which)
+    for g in range(2):
+        begin(g)
+        if g + 2 < EARLY:
+            send_own(0, g + 2)
+
+    all_of(1, rb0, 0).wait_recv()
+    late_lines[0] = rb0[...].reshape(slots, early + 128)
+    for copy in corrections:
+        copy.start()
+    arrived = rb0[:, :, early:].reshape(slots, 128)
+
+    def node_of(numbers):
+        numbers = numbers.astype(F32)
+        return numbers[:, 0:1] * 16.0 + numbers[:, 64:65] - 1.0
+
+    def selection(numbers):
+        return one_hot(iota((rows, slots), 0) == to_row(node_of(numbers), slots).astype(jnp.int32))
+
+    scatter[:, 2 * lines :] = selection(arrived)
+
+    all_of(1, rb1, 1).wait_recv()
+    for g in range(EARLY, GROUPS):
+        set_near(hist_near[0, :, g * width : (g + 1) * width])
+        rhs[2 * lines :] = rb1[:, :, (g - EARLY) * width : (g - EARLY + 1) * width].reshape(slots, width)
+        inject(0, g, v[g], dot(scatter[...], rhs[...]))
+        send_own(0, g)
+
+    for g in range(2, EARLY):
+        begin(g)
+    for copy, on in zip(corrections, corrections_on):
+        copy.wait_recv()
+        on.start()
+    all_of(0, ra2, 2).wait_recv()
+    ob2[...] = turn(ra2[...])
+    send_hop(1, ob2, rb2, 2)
+    gather[lines:] = one_hot(iota((slots, rows), 1) == node_of(dot(swap[...], arrived)).astype(jnp.int32))
+
+    def choose(place):
+        chosen = dot(zr[:, place * rows : (place + 1) * rows], selection(late_lines[place, :, early:]))
+        selected[:, place * slots : (place + 1) * slots] = chosen.astype(BF16)
+
+    for place in range(3):
+        choose(place)
 
     def finish(item):
         step, g = item // GROUPS, lax.rem(item, GROUPS)
         pair, side = g // 2, lax.rem(g, 2)
         at = pl.ds(pl.multiple_of(g * width, width), width)
         in_half = pl.ds(pl.multiple_of(side * width, width), width)
+        v[g] = dot(zr[:, : 3 * rows], x[step, g, : 3 * rows])
         whole(step, g, 1, far_sem).wait_recv()
         v[g] += dot(zr[:, 3 * rows :], x[step, g, 3 * rows :])
 
+        @pl.when((step == 0) & (g == 0))
+        def _():
+            for copy in corrections_on:
+                copy.wait_recv()
+            choose(3)
+
+        @pl.when((step == 0) & (g < EARLY))
+        def _():
+            at = pl.ds(pl.multiple_of(lax.rem(g, EARLY) * width, width), width)
+            v[g] += dot(selected[...], late_lines[:, :, at].reshape(4 * slots, width))
+
         @pl.when(step == 0)
         def _():
             @pl.when(g == 0)
             def _():
-                wait_zones(rb2, 2)
+                all_of(1, rb2, 2).wait_recv()
 
             set_near(hist_near[1, :, at])
             rhs[2 * lines :] = rb2[:, :, at].reshape(slots, width)
@@ -355,7 +394,7 @@
 
             @pl.when(side == 0)
             def _():
-                wait_zones(rb.at[which], 3 + which)
+                all_of(1, rb.at[which], 3 + which).wait_recv()
 
             rhs[2 * lines :] = rb[which, :, :block_b, in_half].reshape(slots, width)
             returned = rb[which, :, block_b:, in_half].reshape(slots, width)
@@ -363,7 +402,8 @@
 
         @pl.when(step < steps - 1)
         def _():
-            inject(step + 1, g, v[g])
+            inject(step + 1, g, v[g], dot(scatter[...], rhs[...]))
+            send_own(step + 1, g)
 
         @pl.when(step == steps - 1)
         def _():
@@ -378,27 +418,24 @@
             near_volts = ends[:lines] + dot(gather[:lines], (volts - top.astype(F32)).astype(BF16))
             history = gain[...] * near_volts - hist_near[step, :, at]
             oa[which, :, :block_a, in_half] = (
-                dot(slots_out[...], history.astype(BF16)).astype(BF16).reshape(subs, block_a, width)
+                dot(slots_out[...], history.astype(BF16)).astype(BF16).reshape(zones, block_a, width)
             )
-            oa[which, :, block_a:, in_half] = ends[lines:].astype(BF16).reshape(subs, block_a, width)
+            oa[which, :, block_a:, in_half] = ends[lines:].astype(BF16).reshape(zones, block_a, width)
 
             @pl.when(side == 1)
             def _():
-                send_subs(oa.at[which], ra.at[which], 3 + which)
+                send_hop(0, oa.at[which], ra.at[which], 3 + which)
 
         @pl.when((side == 0) & (item >= 2) & (item < 2 + 4 * 2))
         def _():
             which = item // 2 - 1
-            wait_subs(ra.at[which], 3 + which)
+            all_of(0, ra.at[which], 3 + which).wait_recv()
             ob[which, :, :block_b] = turn(ra[which, :, :block_a])
             ob[which, :, block_b:] = turn(ra[which, :, block_a:])
-            send_zones(ob.at[which], rb.at[which], 3 + which)
-
-    for item in range(AHEAD):
-        begin(item)
+            send_hop(1, ob.at[which], rb.at[which], 3 + which)
 
     def body(item, carry):
-        @pl.when(item + AHEAD < items)
+        @pl.when((item + AHEAD < items) & (item + AHEAD >= EARLY))
         def _():
             begin(item + AHEAD)
 
@@ -415,11 +452,13 @@
     for g in range(GROUPS):
         whole(steps - 1, g, 3, far_sem).wait_send()
     for which, (sent_a, sent_b) in enumerate(((oa0, ob0), (oa1, ob1), (oa2, ob2))):
-        all_of(sent_a, which, 0, "sub", subs).wait_send()
-        all_of(sent_b, which, 1, "zone", zones).wait_send()
+        all_of(0, sent_a, which).wait_send()
+        all_of(1, sent_b, which).wait_send()
     for which in range(4):
-        all_of(oa.at[which], 3 + which, 0, "sub", subs).wait_send()
-        all_of(ob.at[which], 3 + which, 1, "zone", zones).wait_send()
+        all_of(0, oa.at[which], 3 + which).wait_send()
+        all_of(1, ob.at[which], 3 + which).wait_send()
+    for copy in corrections + corrections_on:
+        copy.wait_send()
     for g in range(GROUPS):
         at = pl.ds(g * width, width)
         pltpu.make_async_copy(v.at[g], out_hbm.at[:, at], out_sem.at[g]).wait()
@@ -444,17 +483,17 @@
     steps, _, rows, cases = sources.shape
     lines = near_node.shape[1]
     slots = 2 * zones * subs
-    block_a, block_b = 2 * zones, 2 * subs
+    block_a, block_b = 2 * subs, 2 * zones
     width = cases // GROUPS
     half = 2 * width
 
     def exchange(wide, tall=1, count=None):
         lead = () if count is None else (count,)
         return [
-            pltpu.VMEM(lead + (subs, tall * block_a, wide), BF16),
-            pltpu.VMEM(lead + (subs, tall * block_a, wide), BF16),
-            pltpu.VMEM(lead + (zones, tall * block_b, wide), BF16),
-            pltpu.VMEM(lead + (zones, tall * block_b, wide), BF16),
+            pltpu.VMEM(lead + (zones, tall * block_a, wide), BF16),
+            pltpu.VMEM(lead + (zones, tall * block_a, wide), BF16),
+            pltpu.VMEM(lead + (subs, tall * block_b, wide), BF16),
+            pltpu.VMEM(lead + (subs, tall * block_b, wide), BF16),
         ]
 
     hbm = pl.BlockSpec(memory_space=pltpu.HBM)
@@ -489,10 +528,14 @@
             pltpu.VMEM((slots, slots), BF16),
             pltpu.VMEM((lines, width), F32),
             pltpu.VMEM((2 * lines + slots, width), BF16),
-            *exchange(half + 128),
-            *exchange(half),
+            *exchange(EARLY * width + 128),
+            *exchange((GROUPS - EARLY) * width),
             *exchange(cases),
             *exchange(half, 2, 4),
+            pltpu.VMEM((4, slots, EARLY * width + 128), BF16),
+            pltpu.VMEM((rows, 4 * slots), BF16),
+            pltpu.SemaphoreType.DMA((4,)),
+            pltpu.SemaphoreType.DMA((4,)),
             pltpu.SemaphoreType.DMA((3 + GROUPS + 4 + 8,)),
             pltpu.SemaphoreType.DMA((steps, GROUPS)),
             pltpu.SemaphoreType.DMA((steps, GROUPS)),

time: 94.9 us -> 90.6 us (0.955)
  Pallas kernels: 92.5 us -> 88.2 us
    pallas_call x1, Pallas kernels: 92.5 us -> 88.2 us  [local(): pl.pallas_call(functools.partial(kernel, zones, subs), out_shape=jax.Shap...]
where the time goes in v3:
time: 90.6 us; the launch traced here: 90.4 us
  Pallas kernels  88.2 us (97%)
  local copies, waits for them, and re-layouts  2.26 us (2%)
    pallas_call x1, Pallas kernels, local(): pl.pallas_call(functools.partial(kernel, zones, subs), out_shape=jax.Shap...  88.2 us
    unnamed x1, local copies, waits for them, and re-layouts  2.26 us

profile of v3, /device:TPU:8, one launch (start us, length us, event | category | flops | bytes accessed | tf_op | source)
XLA Modules:
  0.0 90.4 jit_solution(7695133428947427514)
XLA Ops:
  0.0 88.2 %shard_map.127 = f32[512,512]{1,0:T(8,128)} custom-call(bf16[512,2048]{1,0:T(8,128)(2,1)} %bitcast.10, bf16[4,512,512]{2,1,0:T(8,128)(2,1)} %bitcast.11, f32[512,512]{1,0:T(8,128)} %bitcast.12, f32[2,64,512]{2,1,0:T(8,128)} %bitcast.13, f32[2,64,512]{2,1,0:T(8,128)} %bitcast.14, s32[4,1,512]{2,1,0:T(1,128)} %rest_0_.1, f32[1,512]{1,0:T(1,128)} %rest_1_.1, ...), custom_call_target="tpu_custom_call" | custom-call | tf_op jit(solution)/shard_map/pallas_call | solution.py:510
  88.2 2.3 %copy.15 = f32[1,512,512]{2,1,0:T(8,128)} copy(f32[1,512,512]{2,1,0:T(8,128)} %bitcast.9) | data formatting | bytes 2097152

commit v4 on v3

--- a/solution.py
+++ b/solution.py
@@ -114,27 +114,6 @@
     my_zone, my_sub, me = (lax.axis_index(name) for name in ("zone", "sub", "row"))
     right, left, across = lax.rem(me + 1, 4), lax.rem(me + 3, 4), lax.rem(me + 2, 4)
 
-    loads = [
-        pltpu.make_async_copy(there, here, load_sem.at[3 + GROUPS + 4 + number])
-        for number, (there, here) in enumerate(zip(small_hbm, small))
-    ]
-    loads.append(pltpu.make_async_copy(far_hbm, hist_far, load_sem.at[0]))
-    loads.append(pltpu.make_async_copy(near_hbm, hist_near, load_sem.at[1]))
-    loads.append(pltpu.make_async_copy(src_hbm, src, load_sem.at[2]))
-    for g in range(GROUPS):
-        loads.append(
-            pltpu.make_async_copy(vs_hbm.at[:, pl.ds(g * width, width)], v.at[g], load_sem.at[3 + g])
-        )
-    for place, origin in enumerate((me, left, right, across)):
-        columns = pl.ds(pl.multiple_of(origin * rows, rows), rows)
-        loads.append(
-            pltpu.make_async_copy(
-                z_hbm.at[:, columns], zr.at[:, pl.ds(place * rows, rows)], load_sem.at[3 + GROUPS + place]
-            )
-        )
-    for load in loads:
-        load.start()
-
     barrier = pltpu.get_barrier_semaphore()
     for neighbour in (left, right):
         pl.semaphore_signal(barrier, inc=1, device_id={"row": neighbour}, device_id_type=MESH)
@@ -143,8 +122,35 @@
     for d in range(1, zones):
         pl.semaphore_signal(barrier, inc=1, device_id={"zone": lax.rem(my_zone + d, zones)}, device_id_type=MESH)
 
-    for load in loads[:8]:
-        load.wait()
+    order = (4, 6, 0, 1, 2, 3, 5, 7)
+    loads = {
+        number: pltpu.make_async_copy(small_hbm[number], small[number], load_sem.at[number]) for number in order
+    }
+    far_load = pltpu.make_async_copy(far_hbm, hist_far, load_sem.at[8])
+    near_load = pltpu.make_async_copy(near_hbm, hist_near, load_sem.at[9])
+    src_load = pltpu.make_async_copy(src_hbm, src, load_sem.at[10])
+    start_loads = [
+        pltpu.make_async_copy(vs_hbm.at[:, pl.ds(g * width, width)], v.at[g], load_sem.at[11 + g])
+        for g in range(GROUPS)
+    ]
+    z_loads = []
+    for place, origin in enumerate((me, left, right, across)):
+        columns = pl.ds(pl.multiple_of(origin * rows, rows), rows)
+        z_loads.append(
+            pltpu.make_async_copy(
+                z_hbm.at[:, columns], zr.at[:, pl.ds(place * rows, rows)], load_sem.at[11 + GROUPS + place]
+            )
+        )
+    loads[4].start()
+    loads[6].start()
+    far_load.start()
+    for number in order[2:]:
+        loads[number].start()
+    for load in [near_load, *start_loads, src_load, *z_loads]:
+        load.start()
+
+    loads[4].wait()
+    loads[6].wait()
 
     target = remote_sub[...].astype(F32)
     target_col = to_column(target, lines)
@@ -203,6 +209,19 @@
         values = got.reshape(slots, got.shape[-1])
         return dot(swap[...], values).astype(BF16).reshape(subs, block_b, got.shape[-1])
 
+    far_load.wait()
+    spread = slots_out[...]
+    oa0[:, :, :early] = dot(spread, hist_far[0, :, :early].astype(BF16)).astype(BF16).reshape(zones, block_a, early)
+    oa0[:, :, early:] = numbers_out.reshape(zones, block_a, 128)
+    pl.semaphore_wait(barrier, 2 + subs - 1 + zones - 1)
+    send_hop(0, oa0, ra0, 0)
+    oa1[...] = dot(spread, hist_far[0, :, early:].astype(BF16)).astype(BF16).reshape(zones, block_a, late)
+    send_hop(0, oa1, ra1, 1)
+
+    for number in order[2:]:
+        loads[number].wait()
+    for load in [near_load, *start_loads, src_load]:
+        load.wait()
     near_row = near_node[...]
     near_col = to_column(near_row.astype(F32), lines).astype(jnp.int32)
     near_matrix = one_hot(iota((rows, lines), 0) == near_row)
@@ -216,14 +235,6 @@
     for step in range(steps):
         switched[step] = jnp.broadcast_to(columns[:, step : step + 1], (rows, width))
 
-    loads[8].wait()
-    spread = slots_out[...]
-    values = dot(spread, hist_far[0].astype(BF16)).astype(BF16)
-    oa0[:, :, :early] = values[:, :early].reshape(zones, block_a, early)
-    oa0[:, :, early:] = numbers_out.reshape(zones, block_a, 128)
-    oa1[...] = values[:, early:].reshape(zones, block_a, late)
-    oa2[...] = dot(spread, hist_far[1].astype(BF16)).astype(BF16).reshape(zones, block_a, cases)
-
     def set_near(history):
         top = history.astype(BF16)
         rhs[:lines] = top
@@ -235,19 +246,21 @@
         conduct = switched[step] + jnp.where(faulted, fault_cond[:, at], 0.0)
         x[step, g, :rows] = (src[step, :, at].astype(F32) + lines_in - conduct * volts).astype(BF16)
 
-    def send_own(step, g):
-        for peer, place, sem in ((right, 1, left_sem), (left, 2, right_sem)):
-            own_copy(step, g, peer, place, sem).start()
-
-    def own_copy(step, g, peer, place, sem):
+    def own_half(step, g, peer, place, sem, side):
+        offset = side * (rows // 2)
         return pltpu.make_async_remote_copy(
-            src_ref=x.at[step, g, pl.ds(0, rows)],
-            dst_ref=x.at[step, g, pl.ds(place * rows, rows)],
+            src_ref=x.at[step, g, pl.ds(offset, rows // 2)],
+            dst_ref=x.at[step, g, pl.ds(place * rows + offset, rows // 2)],
             send_sem=send_sem.at[step, g],
-            recv_sem=sem.at[step, g],
+            recv_sem=sem.at[step, g, side],
             device_id={"row": peer},
             device_id_type=MESH,
         )
+
+    def send_own(step, g):
+        for half_of in range(2):
+            own_half(step, g, right, 1, left_sem, half_of).start()
+            own_half(step, g, left, 2, right_sem, 1 - half_of).start()
 
     def pass_on(step, g, peer, place, offset):
         return pltpu.make_async_remote_copy(
@@ -272,88 +285,107 @@
 
     def begin(item):
         step, g = item // GROUPS, lax.rem(item, GROUPS)
-        whole(step, g, 1, left_sem).wait_recv()
+        own_half(step, g, right, 1, left_sem, 0).wait_recv()
         pass_on(step, g, right, 1, 0).start()
-        whole(step, g, 1, right_sem).wait_recv()
+        own_half(step, g, left, 2, right_sem, 1).wait_recv()
         pass_on(step, g, left, 2, rows // 2).start()
 
-    def correct(peer, place, sem):
+    def correct(piece, peer, place):
+        part = pl.ds(16 if piece else 0, slots if piece else 16 + slots)
         return pltpu.make_async_remote_copy(
-            src_ref=late_lines.at[0],
-            dst_ref=late_lines.at[place],
-            send_sem=fix_send.at[place - 1],
-            recv_sem=sem,
+            src_ref=late_lines.at[0, piece, part],
+            dst_ref=late_lines.at[place, piece, part],
+            send_sem=fix_send.at[piece, place - 1],
+            recv_sem=fix_recv.at[piece, place - 1],
             device_id={"row": peer},
             device_id_type=MESH,
         )
 
-    def correct_on(peer, place, offset):
+    def correct_on(piece, peer, place):
+        middle = 16 + slots // 2
+        first = 16 if piece else 0
+        part = pl.ds(first, middle - first) if place == 1 else pl.ds(middle, slots // 2)
         return pltpu.make_async_remote_copy(
-            src_ref=late_lines.at[place, pl.ds(offset, slots // 2)],
-            dst_ref=late_lines.at[3, pl.ds(offset, slots // 2)],
-            send_sem=fix_send.at[place + 1],
-            recv_sem=fix_recv.at[place + 1],
+            src_ref=late_lines.at[place, piece, part],
+            dst_ref=late_lines.at[3, piece, part],
+            send_sem=fix_send.at[piece, place + 1],
+            recv_sem=fix_recv.at[piece, place + 1],
             device_id={"row": peer},
             device_id_type=MESH,
         )
 
-    corrections = (correct(right, 1, fix_recv.at[0]), correct(left, 2, fix_recv.at[1]))
-    corrections_on = (correct_on(right, 1, 0), correct_on(left, 2, slots // 2))
-
-    for load in loads[9:]:
-        load.wait()
-    for g in range(EARLY):
+    corrections = [(correct(piece, right, 1), correct(piece, left, 2)) for piece in range(EARLY)]
+    corrections_on = [(correct_on(piece, right, 1), correct_on(piece, left, 2)) for piece in range(EARLY)]
+
+    def correct_relay(piece):
+        for copy, on in zip(corrections[piece], corrections_on[piece]):
+            copy.wait_recv()
+            on.start()
+
+    def near_lines(g):
         set_near(hist_near[0, :, g * width : (g + 1) * width])
+
+    for g in range(2):
+        near_lines(g)
         inject(0, g, v[g], dot(scatter[:, : 2 * lines], rhs[: 2 * lines]))
-    pl.semaphore_wait(barrier, 2 + subs - 1 + zones - 1)
-    send_hop(0, oa0, ra0, 0)
-    for g in range(2):
         send_own(0, g)
-    send_hop(0, oa1, ra1, 1)
-    send_hop(0, oa2, ra2, 2)
     for which, (got, out, last) in enumerate(((ra0, ob0, rb0), (ra1, ob1, rb1))):
         all_of(0, got, which).wait_recv()
         out[...] = turn(got[...])
         send_hop(1, out, last, which)
+    oa2[...] = dot(spread, hist_far[1].astype(BF16)).astype(BF16).reshape(zones, block_a, cases)
+    send_hop(0, oa2, ra2, 2)
+    for g in range(2, EARLY):
+        near_lines(g)
+        inject(0, g, v[g], dot(scatter[:, : 2 * lines], rhs[: 2 * lines]))
     for g in range(2):
         begin(g)
         if g + 2 < EARLY:
             send_own(0, g + 2)
 
     all_of(1, rb0, 0).wait_recv()
-    late_lines[0] = rb0[...].reshape(slots, early + 128)
-    for copy in corrections:
-        copy.start()
     arrived = rb0[:, :, early:].reshape(slots, 128)
-
-    def node_of(numbers):
-        numbers = numbers.astype(F32)
-        return numbers[:, 0:1] * 16.0 + numbers[:, 64:65] - 1.0
-
-    def selection(numbers):
-        return one_hot(iota((rows, slots), 0) == to_row(node_of(numbers), slots).astype(jnp.int32))
-
-    scatter[:, 2 * lines :] = selection(arrived)
-
-    all_of(1, rb1, 1).wait_recv()
-    for g in range(EARLY, GROUPS):
-        set_near(hist_near[0, :, g * width : (g + 1) * width])
-        rhs[2 * lines :] = rb1[:, :, (g - EARLY) * width : (g - EARLY + 1) * width].reshape(slots, width)
-        inject(0, g, v[g], dot(scatter[...], rhs[...]))
-        send_own(0, g)
-
-    for g in range(2, EARLY):
-        begin(g)
-    for copy, on in zip(corrections, corrections_on):
-        copy.wait_recv()
-        on.start()
+    numbers = arrived.astype(F32)
+    high_row, low_row = to_row(numbers[:, 0:1], slots), to_row(numbers[:, 64:65], slots)
+    place_of = iota((16, slots), 0)
+    node_rows = jnp.where(place_of == 0, high_row, jnp.where(place_of == 1, low_row, 0.0))
+    late_lines[0, 0, :16, :slots] = node_rows.astype(BF16)
+    for piece in range(EARLY):
+        late_lines[0, piece, 16:] = rb0[:, :, piece * width : (piece + 1) * width].reshape(slots, width)
+        for copy in corrections[piece]:
+            copy.start()
+
+    def selection(place):
+        numbers = late_lines[place, 0, :16, :slots].astype(F32)
+        node = (numbers[0:1] * 16.0 + numbers[1:2] - 1.0).astype(jnp.int32)
+        return one_hot(iota((rows, slots), 0) == node)
+
     all_of(0, ra2, 2).wait_recv()
     ob2[...] = turn(ra2[...])
     send_hop(1, ob2, rb2, 2)
-    gather[lines:] = one_hot(iota((slots, rows), 1) == node_of(dot(swap[...], arrived)).astype(jnp.int32))
+    scatter[:, 2 * lines :] = selection(0)
+
+    all_of(1, rb1, 1).wait_recv()
+    for g in range(EARLY, GROUPS):
+        near_lines(g)
+        rhs[2 * lines :] = rb1[:, :, (g - EARLY) * width : (g - EARLY + 1) * width].reshape(slots, width)
+        inject(0, g, v[g], dot(scatter[...], rhs[...]))
+    for g in range(GROUPS):
+        if g < EARLY:
+            correct_relay(g)
+        if EARLY + g < GROUPS:
+            send_own(0, EARLY + g)
+
+    for g in range(2, EARLY):
+        begin(g)
+    turned = dot(swap[...], arrived)
+    node_col = turned[:, 0:1] * 16.0 + turned[:, 64:65] - 1.0
+    gather[lines:] = one_hot(iota((slots, rows), 1) == node_col.astype(jnp.int32))
+    for load in z_loads:
+        load.wait()
 
     def choose(place):
-        chosen = dot(zr[:, place * rows : (place + 1) * rows], selection(late_lines[place, :, early:]))
+        chosen = dot(zr[:, place * rows : (place + 1) * rows], selection(place))
         selected[:, place * slots : (place + 1) * slots] = chosen.astype(BF16)
 
     for place in range(3):
@@ -364,20 +396,26 @@
         pair, side = g // 2, lax.rem(g, 2)
         at = pl.ds(pl.multiple_of(g * width, width), width)
         in_half = pl.ds(pl.multiple_of(side * width, width), width)
+        own_half(step, g, right, 1, left_sem, 1).wait_recv()
+        own_half(step, g, left, 2, right_sem, 0).wait_recv()
         v[g] = dot(zr[:, : 3 * rows], x[step, g, : 3 * rows])
         whole(step, g, 1, far_sem).wait_recv()
         v[g] += dot(zr[:, 3 * rows :], x[step, g, 3 * rows :])
 
         @pl.when((step == 0) & (g == 0))
         def _():
-            for copy in corrections_on:
+            for copy in corrections_on[0]:
                 copy.wait_recv()
             choose(3)
 
-        @pl.when((step == 0) & (g < EARLY))
-        def _():
-            at = pl.ds(pl.multiple_of(lax.rem(g, EARLY) * width, width), width)
-            v[g] += dot(selected[...], late_lines[:, :, at].reshape(4 * slots, width))
+        for piece in range(EARLY):
+
+            @pl.when((step == 0) & (g == piece))
+            def _():
+                if piece:
+                    for copy in corrections_on[piece]:
+                        copy.wait_recv()
+                v[g] += dot(selected[...], late_lines[:, piece, 16:].reshape(4 * slots, width))
 
         @pl.when(step == 0)
         def _():
@@ -457,8 +495,9 @@
     for which in range(4):
         all_of(0, oa.at[which], 3 + which).wait_send()
         all_of(1, ob.at[which], 3 + which).wait_send()
-    for copy in corrections + corrections_on:
-        copy.wait_send()
+    for pair in corrections + corrections_on:
+        for copy in pair:
+            copy.wait_send()
     for g in range(GROUPS):
         at = pl.ds(g * width, width)
         pltpu.make_async_copy(v.at[g], out_hbm.at[:, at], out_sem.at[g]).wait()
@@ -532,14 +571,14 @@
             *exchange((GROUPS - EARLY) * width),
             *exchange(cases),
             *exchange(half, 2, 4),
-            pltpu.VMEM((4, slots, EARLY * width + 128), BF16),
+            pltpu.VMEM((4, EARLY, 16 + slots, width), BF16),
             pltpu.VMEM((rows, 4 * slots), BF16),
-            pltpu.SemaphoreType.DMA((4,)),
-            pltpu.SemaphoreType.DMA((4,)),
-            pltpu.SemaphoreType.DMA((3 + GROUPS + 4 + 8,)),
+            pltpu.SemaphoreType.DMA((EARLY, 4)),
+            pltpu.SemaphoreType.DMA((EARLY, 4)),
+            pltpu.SemaphoreType.DMA((11 + GROUPS + 4,)),
             pltpu.SemaphoreType.DMA((steps, GROUPS)),
-            pltpu.SemaphoreType.DMA((steps, GROUPS)),
-            pltpu.SemaphoreType.DMA((steps, GROUPS)),
+            pltpu.SemaphoreType.DMA((steps, GROUPS, 2)),
+            pltpu.SemaphoreType.DMA((steps, GROUPS, 2)),
             pltpu.SemaphoreType.DMA((steps, GROUPS)),
             pltpu.SemaphoreType.DMA((7, 2)),
             pltpu.SemaphoreType.DMA((7, 2)),

time: 90.6 us -> 87.8 us (0.969)
  Pallas kernels: 88.2 us -> 85.4 us
    pallas_call x1, Pallas kernels: 88.2 us -> 85.4 us  [local(): pl.pallas_call(functools.partial(kernel, zones, subs), out_shape=jax.Shap...]
where the time goes in v4:
time: 87.8 us; the launch traced here: 87.7 us
  Pallas kernels  85.4 us (97%)
  local copies, waits for them, and re-layouts  2.26 us (3%)
    pallas_call x1, Pallas kernels, local(): pl.pallas_call(functools.partial(kernel, zones, subs), out_shape=jax.Shap...  85.4 us
    unnamed x1, local copies, waits for them, and re-layouts  2.26 us

profile of v4, /device:TPU:8, one launch (start us, length us, event | category | flops | bytes accessed | tf_op | source)
XLA Modules:
  0.0 87.7 jit_solution(7894533424579198874)
XLA Ops:
  0.0 85.4 %shard_map.127 = f32[512,512]{1,0:T(8,128)} custom-call(bf16[512,2048]{1,0:T(8,128)(2,1)} %bitcast.10, bf16[4,512,512]{2,1,0:T(8,128)(2,1)} %bitcast.11, f32[512,512]{1,0:T(8,128)} %bitcast.12, f32[2,64,512]{2,1,0:T(8,128)} %bitcast.13, f32[2,64,512]{2,1,0:T(8,128)} %bitcast.14, s32[4,1,512]{2,1,0:T(1,128)} %rest_0_.1, f32[1,512]{1,0:T(1,128)} %rest_1_.1, ...), custom_call_target="tpu_custom_call" | custom-call | tf_op jit(solution)/shard_map/pallas_call | solution.py:549
  85.4 2.3 %copy.15 = f32[1,512,512]{2,1,0:T(8,128)} copy(f32[1,512,512]{2,1,0:T(8,128)} %bitcast.9) | data formatting | bytes 2097152

commit v5 on v4

--- a/solution.py
+++ b/solution.py
@@ -47,7 +47,7 @@
     far_hbm,
     *rest,
 ):
-    small_hbm, out_hbm, small, rest = rest[:8], rest[8], rest[9:17], rest[17:]
+    small_hbm, out_ref, small, rest = rest[:8], rest[8], rest[9:17], rest[17:]
     (
         switch_on,
         switch_cond,
@@ -108,7 +108,6 @@
     slots = 2 * zones * subs
     block_a, block_b = 2 * subs, 2 * zones
     width = cases // GROUPS
-    half = 2 * width
     early, late = EARLY * width, (GROUPS - EARLY) * width
     items = steps * GROUPS
     my_zone, my_sub, me = (lax.axis_index(name) for name in ("zone", "sub", "row"))
@@ -393,9 +392,7 @@
 
     def finish(item):
         step, g = item // GROUPS, lax.rem(item, GROUPS)
-        pair, side = g // 2, lax.rem(g, 2)
         at = pl.ds(pl.multiple_of(g * width, width), width)
-        in_half = pl.ds(pl.multiple_of(side * width, width), width)
         own_half(step, g, right, 1, left_sem, 1).wait_recv()
         own_half(step, g, left, 2, right_sem, 0).wait_recv()
         v[g] = dot(zr[:, : 3 * rows], x[step, g, : 3 * rows])
@@ -428,14 +425,10 @@
 
         @pl.when((step == 1) | (step == 2))
         def _():
-            which = (step - 1) * 2 + pair
-
-            @pl.when(side == 0)
-            def _():
-                all_of(1, rb.at[which], 3 + which).wait_recv()
-
-            rhs[2 * lines :] = rb[which, :, :block_b, in_half].reshape(slots, width)
-            returned = rb[which, :, block_b:, in_half].reshape(slots, width)
+            which = item - GROUPS
+            all_of(1, rb.at[which], 3 + which).wait_recv()
+            rhs[2 * lines :] = rb[which, :, :block_b].reshape(slots, width)
+            returned = rb[which, :, block_b:].reshape(slots, width)
             set_near(gain[...] * dot(slots_back[...], returned) - hist_far[step - 1, :, at])
 
         @pl.when(step < steps - 1)
@@ -445,28 +438,24 @@
 
         @pl.when(step == steps - 1)
         def _():
-            pltpu.make_async_copy(v.at[g], out_hbm.at[:, at], out_sem.at[g]).start()
+            pltpu.make_async_copy(v.at[g], out_ref.at[:, at], out_sem.at[g]).start()
 
         @pl.when(step < 2)
         def _():
-            which = step * 2 + pair
             volts = v[g]
             top = volts.astype(BF16)
             ends = dot(gather[...], top)
             near_volts = ends[:lines] + dot(gather[:lines], (volts - top.astype(F32)).astype(BF16))
             history = gain[...] * near_volts - hist_near[step, :, at]
-            oa[which, :, :block_a, in_half] = (
+            oa[item, :, :block_a] = (
                 dot(slots_out[...], history.astype(BF16)).astype(BF16).reshape(zones, block_a, width)
             )
-            oa[which, :, block_a:, in_half] = ends[lines:].astype(BF16).reshape(zones, block_a, width)
-
-            @pl.when(side == 1)
-            def _():
-                send_hop(0, oa.at[which], ra.at[which], 3 + which)
-
-        @pl.when((side == 0) & (item >= 2) & (item < 2 + 4 * 2))
-        def _():
-            which = item // 2 - 1
+            oa[item, :, block_a:] = ends[lines:].astype(BF16).reshape(zones, block_a, width)
+            send_hop(0, oa.at[item], ra.at[item], 3 + item)
+
+        @pl.when((item >= 1) & (item < 1 + 2 * GROUPS))
+        def _():
+            which = item - 1
             all_of(0, ra.at[which], 3 + which).wait_recv()
             ob[which, :, :block_b] = turn(ra[which, :, :block_a])
             ob[which, :, block_b:] = turn(ra[which, :, block_a:])
@@ -492,7 +481,7 @@
     for which, (sent_a, sent_b) in enumerate(((oa0, ob0), (oa1, ob1), (oa2, ob2))):
         all_of(0, sent_a, which).wait_send()
         all_of(1, sent_b, which).wait_send()
-    for which in range(4):
+    for which in range(2 * GROUPS):
         all_of(0, oa.at[which], 3 + which).wait_send()
         all_of(1, ob.at[which], 3 + which).wait_send()
     for pair in corrections + corrections_on:
@@ -500,7 +489,7 @@
             copy.wait_send()
     for g in range(GROUPS):
         at = pl.ds(g * width, width)
-        pltpu.make_async_copy(v.at[g], out_hbm.at[:, at], out_sem.at[g]).wait()
+        pltpu.make_async_copy(v.at[g], out_ref.at[:, at], out_sem.at[g]).wait()
 
 
 def local(zones, subs, *arguments):
@@ -524,7 +513,6 @@
     slots = 2 * zones * subs
     block_a, block_b = 2 * subs, 2 * zones
     width = cases // GROUPS
-    half = 2 * width
 
     def exchange(wide, tall=1, count=None):
         lead = () if count is None else (count,)
@@ -548,9 +536,9 @@
     )
     result = pl.pallas_call(
         functools.partial(kernel, zones, subs),
-        out_shape=jax.ShapeDtypeStruct((rows, cases), F32),
+        out_shape=pltpu.VMEM((rows, cases), F32),
         in_specs=[hbm] * (5 + len(small)),
-        out_specs=hbm,
+        out_specs=pl.BlockSpec(memory_space=pl.ANY),
         scratch_shapes=[
             *(pltpu.VMEM(array.shape, array.dtype) for array in small),
             pltpu.VMEM((rows, 4 * rows), BF16),
@@ -570,7 +558,7 @@
             *exchange(EARLY * width + 128),
             *exchange((GROUPS - EARLY) * width),
             *exchange(cases),
-            *exchange(half, 2, 4),
+            *exchange(width, 2, 2 * GROUPS),
             pltpu.VMEM((4, EARLY, 16 + slots, width), BF16),
             pltpu.VMEM((rows, 4 * slots), BF16),
             pltpu.SemaphoreType.DMA((EARLY, 4)),
@@ -580,8 +568,8 @@
             pltpu.SemaphoreType.DMA((steps, GROUPS, 2)),
             pltpu.SemaphoreType.DMA((steps, GROUPS, 2)),
             pltpu.SemaphoreType.DMA((steps, GROUPS)),
-            pltpu.SemaphoreType.DMA((7, 2)),
-            pltpu.SemaphoreType.DMA((7, 2)),
+            pltpu.SemaphoreType.DMA((3 + 2 * GROUPS, 2)),
+            pltpu.SemaphoreType.DMA((3 + 2 * GROUPS, 2)),
             pltpu.SemaphoreType.DMA((GROUPS,)),
         ],
         compiler_params=pltpu.CompilerParams(

time: 87.8 us -> 85.8 us (0.977)
  local copies, waits for them, and re-layouts: 2.26 us -> 0.97 us
  Pallas kernels: 85.4 us -> 84.4 us
    unnamed x1, local copies, waits for them, and re-layouts: 2.26 us -> 0.97 us
    pallas_call x1, Pallas kernels: 85.4 us -> 84.4 us  [local(): pl.pallas_call(functools.partial(kernel, zones, subs), out_shape=pltpu.VM...]
where the time goes in v5:
time: 85.8 us; the launch traced here: 85.4 us
  Pallas kernels  84.4 us (98%)
  local copies, waits for them, and re-layouts  0.97 us (1%)
    pallas_call x1, Pallas kernels, local(): pl.pallas_call(functools.partial(kernel, zones, subs), out_shape=pltpu.VM...  84.4 us

profile of v5, /device:TPU:8, one launch (start us, length us, event | category | flops | bytes accessed | tf_op | source)
XLA Modules:
  0.0 85.4 jit_solution(13651059779506192469)
XLA Ops:
  0.0 84.4 %shard_map.127 = f32[512,512]{1,0:T(8,128)S(1)} custom-call(bf16[512,2048]{1,0:T(8,128)(2,1)} %bitcast.10, bf16[4,512,512]{2,1,0:T(8,128)(2,1)} %bitcast.11, f32[512,512]{1,0:T(8,128)} %bitcast.12, f32[2,64,512]{2,1,0:T(8,128)} %bitcast.13, f32[2,64,512]{2,1,0:T(8,128)} %bitcast.14, s32[4,1,512]{2,1,0:T(1,128)} %rest_0_.1, f32[1,512]{1,0:T(1,128)} %rest_1_.1, ...), custom_call_target="tpu_custom_call" | custom-call | tf_op jit(solution)/shard_map/pallas_call | solution.py:537
  84.4 1.0 %copy.15 = f32[1,512,512]{2,1,0:T(8,128)} copy(f32[1,512,512]{2,1,0:T(8,128)S(1)} %bitcast.9) | data formatting | bytes 2097152

commit v6 on v5

--- a/solution.py
+++ b/solution.py
@@ -100,7 +100,6 @@
         far_sem,
         ex_send,
         ex_recv,
-        out_sem,
     ) = rest
     rows, nodes = z_hbm.shape
     steps, _, cases = src_hbm.shape
@@ -438,7 +437,7 @@
 
         @pl.when(step == steps - 1)
         def _():
-            pltpu.make_async_copy(v.at[g], out_ref.at[:, at], out_sem.at[g]).start()
+            out_ref[:, at] = v[g]
 
         @pl.when(step < 2)
         def _():
@@ -462,6 +461,18 @@
             send_hop(1, ob.at[which], rb.at[which], 3 + which)
 
     def body(item, carry):
+        @pl.when(item == items - 3)
+        def _():
+            for which, (sent_a, sent_b) in enumerate(((oa0, ob0), (oa1, ob1), (oa2, ob2))):
+                all_of(0, sent_a, which).wait_send()
+                all_of(1, sent_b, which).wait_send()
+            for which in range(2 * GROUPS):
+                all_of(0, oa.at[which], 3 + which).wait_send()
+                all_of(1, ob.at[which], 3 + which).wait_send()
+            for pair in corrections + corrections_on:
+                for copy in pair:
+                    copy.wait_send()
+
         @pl.when((item + AHEAD < items) & (item + AHEAD >= EARLY))
         def _():
             begin(item + AHEAD)
@@ -478,18 +489,6 @@
 
     for g in range(GROUPS):
         whole(steps - 1, g, 3, far_sem).wait_send()
-    for which, (sent_a, sent_b) in enumerate(((oa0, ob0), (oa1, ob1), (oa2, ob2))):
-        all_of(0, sent_a, which).wait_send()
-        all_of(1, sent_b, which).wait_send()
-    for which in range(2 * GROUPS):
-        all_of(0, oa.at[which], 3 + which).wait_send()
-        all_of(1, ob.at[which], 3 + which).wait_send()
-    for pair in corrections + corrections_on:
-        for copy in pair:
-            copy.wait_send()
-    for g in range(GROUPS):
-        at = pl.ds(g * width, width)
-        pltpu.make_async_copy(v.at[g], out_ref.at[:, at], out_sem.at[g]).wait()
 
 
 def local(zones, subs, *arguments):
@@ -538,7 +537,7 @@
         functools.partial(kernel, zones, subs),
         out_shape=pltpu.VMEM((rows, cases), F32),
         in_specs=[hbm] * (5 + len(small)),
-        out_specs=pl.BlockSpec(memory_space=pl.ANY),
+        out_specs=pl.BlockSpec(memory_space=pltpu.VMEM),
         scratch_shapes=[
             *(pltpu.VMEM(array.shape, array.dtype) for array in small),
             pltpu.VMEM((rows, 4 * rows), BF16),
@@ -570,7 +569,6 @@
             pltpu.SemaphoreType.DMA((steps, GROUPS)),
             pltpu.SemaphoreType.DMA((3 + 2 * GROUPS, 2)),
             pltpu.SemaphoreType.DMA((3 + 2 * GROUPS, 2)),
-            pltpu.SemaphoreType.DMA((GROUPS,)),
         ],
         compiler_params=pltpu.CompilerParams(
             collective_id=0, has_side_effects=True, vmem_limit_bytes=56 * 1024 * 1024

time: 85.8 us -> 85.7 us (level)
  no operation moved by 1% of the time
where the time goes in v6:
time: 85.7 us; the launch traced here: 85.3 us
  Pallas kernels  84.4 us (98%)
  local copies, waits for them, and re-layouts  0.97 us (1%)
    pallas_call x1, Pallas kernels, local(): pl.pallas_call(functools.partial(kernel, zones, subs), out_shape=pltpu.VM...  84.4 us

profile of v6, /device:TPU:8, one launch (start us, length us, event | category | flops | bytes accessed | tf_op | source)
XLA Modules:
  0.0 85.3 jit_solution(7817607408015150624)
XLA Ops:
  0.0 84.4 %shard_map.127 = f32[512,512]{1,0:T(8,128)S(1)} custom-call(bf16[512,2048]{1,0:T(8,128)(2,1)} %bitcast.10, bf16[4,512,512]{2,1,0:T(8,128)(2,1)} %bitcast.11, f32[512,512]{1,0:T(8,128)} %bitcast.12, f32[2,64,512]{2,1,0:T(8,128)} %bitcast.13, f32[2,64,512]{2,1,0:T(8,128)} %bitcast.14, s32[4,1,512]{2,1,0:T(1,128)} %rest_0_.1, f32[1,512]{1,0:T(1,128)} %rest_1_.1, ...), custom_call_target="tpu_custom_call" | custom-call | tf_op jit(solution)/shard_map/pallas_call | solution.py:536
  84.4 1.0 %copy.15 = f32[1,512,512]{2,1,0:T(8,128)} copy(f32[1,512,512]{2,1,0:T(8,128)S(1)} %bitcast.9) | data formatting | bytes 2097152
